TPU v7x, 128 devices: a whole 4x4x4 slice. The times are simulated.
128 devices in a mesh: pipe: 2 (over x_lo), tensor: 4 (over x_hi, core), dp: 16 (over z, y).
Axes of the slice: x: 4 (x_hi: 2, x_lo: 2; x = x_hi * 2 + x_lo), y: 4, z: 4, core: 2. Of those that a mesh axis runs over, the one named last changes fastest.
Arguments:
- layer_inputs: bfloat16 [2, 2048, 8192], P('pipe', 'dp', 'tensor'), may hold values from -6 to 6
- norm_gain: float32 [2, 8192], P('pipe', 'tensor'), may hold values from 0.25 to 1.75
- value_weight: bfloat16 [2, 8192, 512], P('pipe', ('tensor', 'dp')), may hold values from -0.0625 to 0.0625
- out_weight: bfloat16 [2, 4096, 8192], P('pipe', None, ('tensor', 'dp')), may hold values from -0.09375 to 0.09375
- scores: bfloat16 [2, 16, 4, 32, 32, 32], P('pipe', 'dp', None, 'tensor'), may hold values from -12 to 312, as said below
- head_weight: bfloat16 [8192], P('tensor'), may hold values from -0.0625 to 0.0625
- lengths: int32 [16, 4], replicated, may hold values from 1 to 32, 112 in all within a row
- returns: float32 [2048], P('dp'), may hold values from 0.5 to 54, as said below
- response_mask: int32 [2048], P('dp'), may hold values 0 or 1
Outputs:
- grad_out: bfloat16 [2, 4096, 8192], P('pipe', None, ('tensor', 'dp'))
- grad_value: bfloat16 [2, 8192, 512], P('pipe', ('tensor', 'dp'))
- grad_gain: float32 [2, 8192], P('pipe', ('tensor', 'dp'))
Inputs may be any that keep to these rules, and one draw needn't show every extreme that they name: `scores`: every query and key pair holds a logit, also above the diagonal and past a microbatch's length; those entries are only removed by the mask of the attention step. Positive returns.
All inputs are finite; a program needn't handle non-finite values. No bound on the sum of `response_mask` on one device may be relied on, other than what follows from the above.
Results may differ from a plain program's by a relative error of at most 0.015.
Values may be sent and summed in bfloat16 or wider, within the bound.
A program may use at most 192 MiB of HBM per device.

v0:
```python
import jax
import jax.numpy as jnp
from jax import lax
from jax.sharding import PartitionSpec as P

D = 8192
HD = 128
KVH = 4


EPS = 1e-05


def passed_along(value, axis, steps):
    count = lax.axis_size(axis)
    initial, last = (max(0, -steps), min(count, count - steps))
    return lax.ppermute(value, axis, [(source, source + steps) for source in range(initial, last)])


def attention_weights(logits, length_row):
    span_len = logits.shape[-1]
    query_place = lax.broadcasted_iota(jnp.int32, (span_len, span_len), 0)
    key_place = lax.broadcasted_iota(jnp.int32, (span_len, span_len), 1)
    allowed = (key_place <= query_place)[None, None] & (
        key_place[None, None] < length_row[:, None, None, None]
    )
    masked = jnp.where(allowed, logits.astype(jnp.float32), -1e30)
    row_top = jnp.max(masked, axis=-1, keepdims=True)
    exponent = jnp.where(allowed, jnp.exp(masked - row_top), 0.0)
    return (exponent / jnp.sum(exponent, axis=-1, keepdims=True)).astype(jnp.bfloat16)


def mix_values(attention, values):
    micro_count, head_count, span_len = attention.shape[:3]
    grouped = attention.astype(jnp.float32).reshape(
        micro_count, KVH, head_count // KVH, span_len, span_len
    )
    values_split = values.astype(jnp.float32).reshape(micro_count, span_len, KVH, HD)
    mixture = jnp.einsum("bgqij,bjgd->bigqd", grouped, values_split)
    return mixture.reshape(micro_count * span_len, head_count * HD).astype(jnp.bfloat16)


def unmix_grads(attention, grad_rows):
    micro_count, head_count, span_len = attention.shape[:3]
    grouped = attention.astype(jnp.float32).reshape(
        micro_count, KVH, head_count // KVH, span_len, span_len
    )
    grad_split = grad_rows.reshape(micro_count, span_len, KVH, head_count // KVH, HD)
    backward = jnp.einsum("bgqij,bigqd->bjgd", grouped, grad_split)
    return backward.reshape(micro_count * span_len, KVH * HD)


def transposed_product(left, right):
    return lax.dot_general(
        left, right, (((1,), (1,)), ((), ())), preferred_element_type=jnp.float32
    )


def leading_product(left, right):
    return lax.dot_general(
        left, right, (((0,), (0,)), ((), ())), preferred_element_type=jnp.float32
    )


def shards(
    layer_inputs,
    norm_gain,
    value_weight,
    out_weight,
    scores,
    head_weight,
    lengths,
    returns,
    response_mask,
):
    section_count = lax.axis_size("pipe")
    section_index = lax.axis_index("pipe")
    replica = lax.axis_index("dp")
    final_section = section_count - 1
    layer_in = layer_inputs[0].astype(jnp.float32)
    row_count, features = layer_in.shape
    gain_row = norm_gain[0]
    value_rows = lax.all_gather(value_weight[0], "dp", axis=0, tiled=True)
    out_cols = lax.all_gather(out_weight[0], "dp", axis=1, tiled=True)
    head_logits = lax.all_gather(scores[0, 0], "tensor", axis=1, tiled=True)
    micro_count = head_logits.shape[0]
    span_len = head_logits.shape[2]
    value_width = value_rows.shape[1]
    own_lengths = lax.dynamic_index_in_dim(lengths, replica, 0, keepdims=False)
    squares = lax.psum(jnp.sum(layer_in * layer_in, axis=-1), "tensor")
    norm_scale = lax.rsqrt(squares / D + EPS)
    normed = (layer_in * norm_scale[:, None] * gain_row).astype(jnp.bfloat16)
    value_sum = lax.psum(jnp.dot(normed, value_rows, preferred_element_type=jnp.float32), "tensor")
    value_round = value_sum.astype(jnp.bfloat16)
    attention = attention_weights(head_logits, own_lengths)
    mixture = mix_values(attention, value_round)

    def project_out(operands):
        return jnp.dot(operands[0], operands[1], preferred_element_type=jnp.float32)

    def skip_out(operands):
        return jnp.zeros((row_count, features), jnp.float32)

    hidden_out = layer_in + lax.cond(
        section_index == final_section, project_out, skip_out, (mixture, out_cols)
    )
    head_row = head_weight.astype(jnp.float32)
    out_squares, out_dot = lax.psum(
        (jnp.sum(hidden_out * hidden_out, axis=-1), jnp.sum(hidden_out * head_row, axis=-1)),
        "tensor",
    )
    out_scale = lax.rsqrt(out_squares / D + EPS)
    critic_value = out_scale * out_dot
    position = jnp.arange(row_count, dtype=jnp.int32)
    block_of = position // span_len
    block_len = jnp.sum(
        jnp.where(
            block_of[:, None] == jnp.arange(micro_count, dtype=jnp.int32)[None, :],
            own_lengths[None, :],
            0,
        ),
        axis=1,
    )
    live_mask = ((position % span_len < block_len) & (response_mask == 1)).astype(jnp.float32)
    live_count, return_total = lax.psum((jnp.sum(live_mask), jnp.sum(live_mask * returns)), "dp")
    live_count = jnp.maximum(live_count, 1.0)
    return_mean = return_total / live_count
    return_var = lax.psum(jnp.sum(live_mask * (returns - return_mean) ** 2), "dp") / live_count
    target = (returns - return_mean) * lax.rsqrt(return_var + EPS)
    value_error = live_mask * (critic_value - target)
    slope = (
        out_scale[:, None] * head_row
        - (out_scale * out_scale * critic_value / D)[:, None] * hidden_out
    )
    top_grads = (
        (value_error[:, None] * slope).astype(jnp.bfloat16).reshape(micro_count, span_len, features)
    )
    layer_blocks = layer_in.reshape(micro_count, span_len, features)
    scale_blocks = norm_scale.reshape(micro_count, span_len)
    sum_blocks = value_sum.reshape(micro_count, span_len, value_width)

    def local_part(operands):
        grad_rows, weights, block_weights = operands
        return unmix_grads(block_weights[None], transposed_product(grad_rows, weights))

    def empty_part(operands):
        return jnp.zeros((span_len, value_width), jnp.float32)

    def tick(tick_index, state_tuple):
        arriving, grads_kept, value_kept, gain_total = state_tuple
        microbatch = tick_index - (final_section - section_index)
        working = (microbatch >= 0) & (microbatch < micro_count)
        current = jnp.clip(microbatch, 0, micro_count - 1)
        upstream = jnp.where(
            section_index == final_section,
            lax.dynamic_index_in_dim(top_grads, current, 0, keepdims=False),
            arriving,
        )
        block_weights = lax.dynamic_index_in_dim(attention, current, 0, keepdims=False)
        partial_grad = lax.cond(
            working, local_part, empty_part, (upstream, out_cols, block_weights)
        )
        value_grad = lax.psum(partial_grad, "tensor").astype(jnp.bfloat16)
        normed_grad = transposed_product(value_grad, value_rows)
        block_in = lax.dynamic_index_in_dim(layer_blocks, current, 0, keepdims=False)
        block_scale = lax.dynamic_index_in_dim(scale_blocks, current, 0, keepdims=False)
        block_sum = lax.dynamic_index_in_dim(sum_blocks, current, 0, keepdims=False)
        inner_term = jnp.sum(value_grad.astype(jnp.float32) * block_sum, axis=-1)
        input_grad = (
            upstream.astype(jnp.float32)
            + block_scale[:, None] * gain_row * normed_grad
            - (block_scale * block_scale * inner_term / D)[:, None] * block_in
        )
        passed = passed_along(input_grad.astype(jnp.bfloat16), "pipe", -1)
        grads_kept = jnp.where(
            working, lax.dynamic_update_index_in_dim(grads_kept, upstream, current, 0), grads_kept
        )
        value_kept = jnp.where(
            working, lax.dynamic_update_index_in_dim(value_kept, value_grad, current, 0), value_kept
        )
        gain_total = gain_total + jnp.where(
            working, jnp.sum(normed_grad * block_in * block_scale[:, None], axis=0), 0.0
        )
        return (passed, grads_kept, value_kept, gain_total)

    start_state = (
        jnp.zeros((span_len, features), jnp.bfloat16),
        jnp.zeros((micro_count, span_len, features), jnp.bfloat16),
        jnp.zeros((micro_count, span_len, value_width), jnp.bfloat16),
        jnp.zeros((features,), jnp.float32),
    )
    finished = lax.fori_loop(0, micro_count + section_count - 1, tick, start_state)
    flat_grads = finished[1].reshape(row_count, features)
    flat_value = finished[2].reshape(row_count, value_width)
    weight_part = leading_product(normed, flat_value)
    value_share, gain_share = (
        lax.psum_scatter(weight_part, "dp", scatter_dimension=0, tiled=True),
        lax.psum_scatter(finished[3], "dp", scatter_dimension=0, tiled=True),
    )
    all_mixture = lax.all_gather(mixture, "dp", axis=0, tiled=True)
    grad_cols = lax.all_to_all(flat_grads, "dp", split_axis=1, concat_axis=0, tiled=True)
    out_share = leading_product(all_mixture, grad_cols)
    return (
        out_share.astype(jnp.bfloat16)[None],
        value_share.astype(jnp.bfloat16)[None],
        gain_share[None],
    )


def solution(mesh):
    return jax.shard_map(
        shards,
        mesh=mesh,
        in_specs=(
            P("pipe", "dp", "tensor"),
            P("pipe", "tensor"),
            P("pipe", ("tensor", "dp"), None),
            P("pipe", None, ("tensor", "dp")),
            P("pipe", "dp", None, "tensor", None, None),
            P("tensor"),
            P(),
            P("dp"),
            P("dp"),
        ),
        out_specs=(
            P("pipe", None, ("tensor", "dp")),
            P("pipe", ("tensor", "dp"), None),
            P("pipe", ("tensor", "dp")),
        ),
        check_vma=False,
    )
```

profile of v0, /device:TPU:0, one launch (start us, length us, event | category | flops | bytes accessed | tf_op | source)
XLA Modules:
  0.0 523.6 jit_solution(4880806649228902959)
XLA Ops:
  9.2 10.0 %psum.62 = f32[128]{0:T(128)S(1)} all-reduce(f32[128]{0:T(128)S(1)} %fusion.22), channel_id=1, replica_groups=mesh['pipe'=2,'tensor'=4,'dp'=16] {'tensor'}, use_global_device_ids=true, to_apply=%region_1.2 | all-reduce | flops 128 | bytes 1024 | tf_op jit(solution)/shard_map/psum | solution.py:90
  19.2 38.7 %all-gather.9.cloned.1.call-done = bf16[1,2048,512]{2,1,0:T(8,128)(2,1)} async-done(((bf16[1,128,512]{2,1,0:T(8,128)(2,1)}), bf16[1,2048,512]{2,1,0:T(8,128)(2,1)}) %all-gather.9.cloned.1.call-update) | async-done | bytes 2097168 | tf_op jit(solution)/shard_map/all_gather | solution.py:83
  62.1 12.2 %all-gather.1 = bf16[1,1,4,32,32,32]{5,3,4,2,1,0:T(8,128)(2,1)S(1)} all-gather(bf16[1,1,4,8,32,32]{5,3,4,2,1,0:T(8,128)(2,1)S(1)} %copy.35), channel_id=3, replica_groups=mesh['pipe'=2,'tensor'=4,'dp'=16] {'tensor'}, dimensions={3}, use_global_device_ids=true | all-gather | bytes 327680 | tf_op jit(solution)/shard_map/all_gather | solution.py:85
  76.5 24.3 %all-reduce.5.cloned.1.call-done = f32[128,512]{1,0:T(8,128)} async-done(((f32[128,512]{1,0:T(8,128)}), f32[128,512]{1,0:T(8,128)}) %all-reduce.5.cloned.1.call-update) | async-done | bytes 262160 | tf_op jit(solution)/shard_map/psum | solution.py:93
  104.8 41.5 %all-reduce.1 = (f32[]{:T(128)}, f32[]{:T(128)}) all-reduce(f32[]{:T(128)} %get-tuple-element.422, f32[]{:T(128)} %get-tuple-element.421), channel_id=1, replica_groups=mesh['pipe'=2,'tensor'=4,'dp'=16] {'dp'}, use_global_device_ids=true, to_apply=%region_13.14 | all-reduce | flops 2 | bytes 16 | tf_op jit(solution)/shard_map/psum | solution.py:125
  148.3 36.9 %psum.68 = f32[]{:T(128)} all-reduce(f32[]{:T(128)} %select_reduce_fusion.1), channel_id=1, replica_groups=mesh['pipe'=2,'tensor'=4,'dp'=16] {'dp'}, use_global_device_ids=true, to_apply=%region_17.18 | all-reduce | flops 1 | bytes 8 | tf_op jit(solution)/shard_map/psum | solution.py:128
  187.1 36.8 %all-gather.11.cloned.1.call-done = bf16[1,4096,2048]{2,1,0:T(8,128)(2,1)} async-done(((bf16[1,4096,128]{2,1,0:T(8,128)(2,1)}), bf16[1,4096,2048]{2,1,0:T(8,128)(2,1)}) %all-gather.11.cloned.1.call-update) | async-done | bytes 16777232 | tf_op jit(solution)/shard_map/all_gather | solution.py:84
  226.7 8.9 %all-reduce.2 = (f32[128]{0:T(128)S(1)}, f32[128]{0:T(128)S(1)}) all-reduce(f32[128]{0:T(128)S(1)} %get-tuple-element.420, f32[128]{0:T(128)S(1)} %get-tuple-element.419), channel_id=1, replica_groups=mesh['pipe'=2,'tensor'=4,'dp'=16] {'tensor'}, use_global_device_ids=true, to_apply=%region_11.12 | all-reduce | flops 256 | bytes 2048 | tf_op jit(solution)/shard_map/psum | solution.py:108
  238.8 195.3 %while.22 = (s32[]{:T(128)}, bf16[32,2048]{1,0:T(8,128)(2,1)S(1)}, bf16[4,32,2048]{2,1,0:T(8,128)(2,1)S(1)}, bf16[4,32,512]{2,1,0:T(8,128)(2,1)}, f32[2048]{0:T(...) while((s32[]{:T(128)}, bf16[32,2048]{1,0:T(8,128)(2,1)S(1)}, ...), condition=%wide.region_24.25_spmd.clone, body=%wide.region_18.24_spmd.clone.sunk | while | flops 613240960 | bytes 22718680 | solution.py:192
  239.8 15.2 %psum.71 = bf16[32,512]{1,0:T(8,128)(2,1)S(1)} all-reduce(f32[32,512]{1,0:T(8,128)S(1)} %get-tuple-element.628), channel_id=1, replica_groups=mesh['pipe'=2,'tensor'=4,'dp'=16] {'tensor'}, use_global_device_ids=true, to_apply=%region_21.21 | all-reduce | flops 16384 | bytes 98304 | tf_op jit(solution)/shard_map/while/body/eval_jaxpr/psum | solution.py:163
  261.0 22.4 %collective-permute-done = bf16[32,2048]{1,0:T(8,128)(2,1)S(1)} collective-permute-done((bf16[32,2048]{1,0:T(8,128)(2,1)}, bf16[32,2048]{1,0:T(8,128)(2,1)S(1)}, u32[]{:S(2)}, u32[]{:S(2)}) %collective-permute-start) | collective-permute-done | bytes 131104 | tf_op jit(solution)/shard_map/while/body/eval_jaxpr/ppermute | solution.py:17
  284.4 12.4 %conditional.5 = (f32[32,512]{1,0:T(8,128)S(1)}) conditional(s32[]{:T(128)} %convert_element_type.179, () %tuple.77, (bf16[32,2048]{1,0:T(8,128)(2,1)S(1)}, bf16[4096,2048]{1,0:T(8,128)(2,1)}, bf16[4,32,32,32]{3,1,2,0:T(8,128)(2,1)}, s32[]{:T(128)}) %tuple.78), branch_computations={%region_19.19_spmd, %region_20.20_spmd} | conditional | flops 545259520 | bytes 18547208 | solution.py:160
  284.4 11.1 %convolution_bitcast_fusion = bf16[4,8,32,128]{3,1,2,0:T(8,128)(2,1)S(1)} fusion(bf16[32,2048]{1,0:T(8,128)(2,1)S(1)} %get-tuple-element.342, bf16[4096,2048]{1,0:T(8,128)(2,1)} %get-tuple-element.343), kind=kOutput, calls=%fused_computation | convolution fusion | flops 536870912 | bytes 17170432 | tf_op jit(solution)/shard_map/while/body/eval_jaxpr/cond/branch_1_fun/dot_general | solution.py:54
  296.8 14.5 %psum.71 = bf16[32,512]{1,0:T(8,128)(2,1)S(1)} all-reduce(f32[32,512]{1,0:T(8,128)S(1)} %get-tuple-element.628), channel_id=1, replica_groups=mesh['pipe'=2,'tensor'=4,'dp'=16] {'tensor'}, use_global_device_ids=true, to_apply=%region_21.21 | all-reduce | flops 16384 | bytes 98304 | tf_op jit(solution)/shard_map/while/body/eval_jaxpr/psum | solution.py:163
  317.4 4.4 collective-permute-done
  322.8 12.1 %conditional.5 = (f32[32,512]{1,0:T(8,128)S(1)}) conditional(s32[]{:T(128)} %convert_element_type.179, () %tuple.77, (bf16[32,2048]{1,0:T(8,128)(2,1)S(1)}, bf16[4096,2048]{1,0:T(8,128)(2,1)}, bf16[4,32,32,32]{3,1,2,0:T(8,128)(2,1)}, s32[]{:T(128)}) %tuple.78), branch_computations={%region_19.19_spmd, %region_20.20_spmd} | conditional | flops 545259520 | bytes 18547208 | solution.py:160
  322.8 10.8 %convolution_bitcast_fusion = bf16[4,8,32,128]{3,1,2,0:T(8,128)(2,1)S(1)} fusion(bf16[32,2048]{1,0:T(8,128)(2,1)S(1)} %get-tuple-element.342, bf16[4096,2048]{1,0:T(8,128)(2,1)} %get-tuple-element.343), kind=kOutput, calls=%fused_computation | convolution fusion | flops 536870912 | bytes 17170432 | tf_op jit(solution)/shard_map/while/body/eval_jaxpr/cond/branch_1_fun/dot_general | solution.py:54
  334.9 14.2 %psum.71 = bf16[32,512]{1,0:T(8,128)(2,1)S(1)} all-reduce(f32[32,512]{1,0:T(8,128)S(1)} %get-tuple-element.628), channel_id=1, replica_groups=mesh['pipe'=2,'tensor'=4,'dp'=16] {'tensor'}, use_global_device_ids=true, to_apply=%region_21.21 | all-reduce | flops 16384 | bytes 98304 | tf_op jit(solution)/shard_map/while/body/eval_jaxpr/psum | solution.py:163
  355.1 4.4 collective-permute-done
  360.4 12.1 %conditional.5 = (f32[32,512]{1,0:T(8,128)S(1)}) conditional(s32[]{:T(128)} %convert_element_type.179, () %tuple.77, (bf16[32,2048]{1,0:T(8,128)(2,1)S(1)}, bf16[4096,2048]{1,0:T(8,128)(2,1)}, bf16[4,32,32,32]{3,1,2,0:T(8,128)(2,1)}, s32[]{:T(128)}) %tuple.78), branch_computations={%region_19.19_spmd, %region_20.20_spmd} | conditional | flops 545259520 | bytes 18547208 | solution.py:160
  360.4 10.8 %convolution_bitcast_fusion = bf16[4,8,32,128]{3,1,2,0:T(8,128)(2,1)S(1)} fusion(bf16[32,2048]{1,0:T(8,128)(2,1)S(1)} %get-tuple-element.342, bf16[4096,2048]{1,0:T(8,128)(2,1)} %get-tuple-element.343), kind=kOutput, calls=%fused_computation | convolution fusion | flops 536870912 | bytes 17170432 | tf_op jit(solution)/shard_map/while/body/eval_jaxpr/cond/branch_1_fun/dot_general | solution.py:54
  372.6 13.7 %psum.71 = bf16[32,512]{1,0:T(8,128)(2,1)S(1)} all-reduce(f32[32,512]{1,0:T(8,128)S(1)} %get-tuple-element.628), channel_id=1, replica_groups=mesh['pipe'=2,'tensor'=4,'dp'=16] {'tensor'}, use_global_device_ids=true, to_apply=%region_21.21 | all-reduce | flops 16384 | bytes 98304 | tf_op jit(solution)/shard_map/while/body/eval_jaxpr/psum | solution.py:163
  392.3 4.5 collective-permute-done
  397.7 12.1 %conditional.5 = (f32[32,512]{1,0:T(8,128)S(1)}) conditional(s32[]{:T(128)} %convert_element_type.179, () %tuple.77, (bf16[32,2048]{1,0:T(8,128)(2,1)S(1)}, bf16[4096,2048]{1,0:T(8,128)(2,1)}, bf16[4,32,32,32]{3,1,2,0:T(8,128)(2,1)}, s32[]{:T(128)}) %tuple.78), branch_computations={%region_19.19_spmd, %region_20.20_spmd} | conditional | flops 545259520 | bytes 18547208 | solution.py:160
  397.7 10.8 %convolution_bitcast_fusion = bf16[4,8,32,128]{3,1,2,0:T(8,128)(2,1)S(1)} fusion(bf16[32,2048]{1,0:T(8,128)(2,1)S(1)} %get-tuple-element.342, bf16[4096,2048]{1,0:T(8,128)(2,1)} %get-tuple-element.343), kind=kOutput, calls=%fused_computation | convolution fusion | flops 536870912 | bytes 17170432 | tf_op jit(solution)/shard_map/while/body/eval_jaxpr/cond/branch_1_fun/dot_general | solution.py:54
  409.9 13.7 %psum.71 = bf16[32,512]{1,0:T(8,128)(2,1)S(1)} all-reduce(f32[32,512]{1,0:T(8,128)S(1)} %get-tuple-element.628), channel_id=1, replica_groups=mesh['pipe'=2,'tensor'=4,'dp'=16] {'tensor'}, use_global_device_ids=true, to_apply=%region_21.21 | all-reduce | flops 16384 | bytes 98304 | tf_op jit(solution)/shard_map/while/body/eval_jaxpr/psum | solution.py:163
  429.5 4.5 collective-permute-done
  434.0 3.6 fusion.31
  438.8 5.2 all-to-all-start
  445.2 41.5 %all-reduce = f32[2048]{0:T(1024)S(1)} all-reduce(f32[2048]{0:T(1024)S(1)} %get-tuple-element.370), channel_id=6, replica_groups=mesh['pipe'=2,'tensor'=4,'dp'=16] {'dp'}, use_global_device_ids=true, to_apply=%region_26.27.clone | all-reduce | flops 2048 | bytes 16384
  487.3 9.3 %fusion.15 = bf16[1,4096,128]{2,1,0:T(8,128)(2,1)} fusion(bf16[2048,4096]{1,0:T(8,128)(2,1)} %all-gather.7.cloned.1.call-done, bf16[2048,128]{1,0:T(8,128)(2,1)S(1)} %bitcast.143), kind=kOutput, calls=%fused_computation.28 | convolution fusion | flops 2148007936 | bytes 18350080 | tf_op jit(solution)/shard_map/dot_general | solution.py:60
  496.6 18.8 %reduce-scatter.2.cloned.1.call-done = f32[128,512]{1,0:T(8,128)} async-done(((f32[2048,512]{1,0:T(8,128)}), f32[128,512]{1,0:T(8,128)}) %reduce-scatter.2.cloned.1.call-update) | async-done | bytes 262160 | tf_op jit(solution)/shard_map/reduce_scatter | solution.py:197
  (123 shorter events, 64.0 us)
Async XLA Ops:
  7.2 54.7 %copy-start = (s32[16,4]{0,1:T(4,128)S(1)}, s32[16,4]{0,1:T(4,128)}, u32[]{:S(2)}) copy-start(s32[16,4]{0,1:T(4,128)} %param.21) | copy-start | bytes 772
  7.2 50.8 %all-gather.9.cloned.1.call-start = ((), (), s32[]{:S(2)}) async-start(), calls=%async_computation.5 | async-start | bytes 2228224 | tf_op jit(solution)/shard_map/all_gather | solution.py:83
  7.9 92.9 %all-reduce.5.cloned.1.call-start = ((), (), s32[]{:S(2)}) async-start(), calls=%async_computation.2 | async-start | bytes 524288 | tf_op jit(solution)/shard_map/psum | solution.py:93
  58.0 3.8 copy-start.7
  61.0 162.9 %all-gather.11.cloned.1.call-start = ((), (), s32[]{:S(2)}) async-start(), calls=%async_computation.6 | async-start | bytes 17825792 | tf_op jit(solution)/shard_map/all_gather | solution.py:84
  61.7 425.5 %all-gather.7.cloned.1.call-start = ((), (), s32[]{:S(2)}) async-start(), calls=%async_computation.3 | async-start | bytes 17825792 | tf_op jit(solution)/shard_map/all_gather | solution.py:200
  76.5 26.2 %copy-start.5 = (bf16[4,32,32,32]{3,1,2,0:T(8,128)(2,1)}, bf16[4,32,32,32]{3,1,2,0:T(8,128)(2,1)S(1)}, u32[]{:S(2)}) copy-start(bf16[4,32,32,32]{3,1,2,0:T(8,128)(2,1)S(1)} %divide_convert_fusion) | copy-start | bytes 786436
  102.7 1.5 copy-start.8
  102.8 1.5 copy-start.10
  102.8 83.2 %copy-start.9 = (bf16[2048]{0:T(1024)(128)(2,1)S(1)}, bf16[2048]{0:T(1024)(128)(2,1)}, u32[]{:S(2)}) copy-start(bf16[2048]{0:T(1024)(128)(2,1)} %param.20) | copy-start | bytes 12292
  102.8 83.2 %copy-start.2 = (bf16[1,128,2048]{2,1,0:T(8,128)(2,1)S(1)}, bf16[1,128,2048]{2,1,0:T(8,128)(2,1)}, u32[]{:S(2)}) copy-start(bf16[1,128,2048]{2,1,0:T(8,128)(2,1)} %param.15) | copy-start | bytes 1572868
  104.1 119.8 %copy-start.3 = (bf16[128,4096]{1,0:T(8,128)(2,1)S(1)}, bf16[128,4096]{1,0:T(8,128)(2,1)}, u32[]{:S(2)}) copy-start(bf16[128,4096]{1,0:T(8,128)(2,1)} %convert_element_type.115) | copy-start | bytes 3145732
  104.1 411.3 %reduce-scatter.2.cloned.1.call-start = ((), (), s32[]{:S(2)}) async-start(), calls=%async_computation.4 | async-start | bytes 4456448 | tf_op jit(solution)/shard_map/reduce_scatter | solution.py:197
  224.0 1.0 copy-start.4
  225.0 13.8 %copy-start.1 = (bf16[1,2048,512]{2,1,0:T(8,128)(2,1)S(1)}, bf16[1,2048,512]{2,1,0:T(8,128)(2,1)}, u32[]{:S(2)}) copy-start(bf16[1,2048,512]{2,1,0:T(8,128)(2,1)} %all-gather.9.cloned.1.call-done) | copy-start | bytes 6291460
  225.0 13.8 %copy-start.6 = (f32[1,2048]{1,0:T(1,128)S(1)}, f32[1,2048]{1,0:T(1,128)}, u32[]{:S(2)}) copy-start(f32[1,2048]{1,0:T(1,128)} %param.16) | copy-start | bytes 24580
  258.3 25.1 %collective-permute-start = (bf16[32,2048]{1,0:T(8,128)(2,1)}, bf16[32,2048]{1,0:T(8,128)(2,1)S(1)}, u32[]{:S(2)}, u32[]{:S(2)}) collective-permute-start(bf16[32,2048]{1,0:T(8,128)(2,1)} %get-tuple-element.567), channel_id=1, source_target_pairs={{64,0},{65,1},{66,2},{67,3},{68,4},{69,5},{70,6},{71,7},{72,8},{73... | collective-permute-start | bytes 393224 | tf_op jit(solution)/shard_map/while/body/eval_jaxpr/ppermute | solution.py:17
  314.7 7.1 %collective-permute-start = (bf16[32,2048]{1,0:T(8,128)(2,1)}, bf16[32,2048]{1,0:T(8,128)(2,1)S(1)}, u32[]{:S(2)}, u32[]{:S(2)}) collective-permute-start(bf16[32,2048]{1,0:T(8,128)(2,1)} %get-tuple-element.567), channel_id=1, source_target_pairs={{64,0},{65,1},{66,2},{67,3},{68,4},{69,5},{70,6},{71,7},{72,8},{73... | collective-permute-start | bytes 393224 | tf_op jit(solution)/shard_map/while/body/eval_jaxpr/ppermute | solution.py:17
  352.4 7.1 %collective-permute-start = (bf16[32,2048]{1,0:T(8,128)(2,1)}, bf16[32,2048]{1,0:T(8,128)(2,1)S(1)}, u32[]{:S(2)}, u32[]{:S(2)}) collective-permute-start(bf16[32,2048]{1,0:T(8,128)(2,1)} %get-tuple-element.567), channel_id=1, source_target_pairs={{64,0},{65,1},{66,2},{67,3},{68,4},{69,5},{70,6},{71,7},{72,8},{73... | collective-permute-start | bytes 393224 | tf_op jit(solution)/shard_map/while/body/eval_jaxpr/ppermute | solution.py:17
  389.6 7.2 %collective-permute-start = (bf16[32,2048]{1,0:T(8,128)(2,1)}, bf16[32,2048]{1,0:T(8,128)(2,1)S(1)}, u32[]{:S(2)}, u32[]{:S(2)}) collective-permute-start(bf16[32,2048]{1,0:T(8,128)(2,1)} %get-tuple-element.567), channel_id=1, source_target_pairs={{64,0},{65,1},{66,2},{67,3},{68,4},{69,5},{70,6},{71,7},{72,8},{73... | collective-permute-start | bytes 393224 | tf_op jit(solution)/shard_map/while/body/eval_jaxpr/ppermute | solution.py:17
  426.9 7.2 %collective-permute-start = (bf16[32,2048]{1,0:T(8,128)(2,1)}, bf16[32,2048]{1,0:T(8,128)(2,1)S(1)}, u32[]{:S(2)}, u32[]{:S(2)}) collective-permute-start(bf16[32,2048]{1,0:T(8,128)(2,1)} %get-tuple-element.567), channel_id=1, source_target_pairs={{64,0},{65,1},{66,2},{67,3},{68,4},{69,5},{70,6},{71,7},{72,8},{73... | collective-permute-start | bytes 393224 | tf_op jit(solution)/shard_map/while/body/eval_jaxpr/ppermute | solution.py:17
  437.7 6.2 %copy-start.11 = (u32[128]{0:T(128)S(1)}, u32[128]{0:T(128)}, u32[]{:S(2)}) copy-start(u32[128]{0:T(128)} %constant.173) | copy-start | bytes 1540
  438.8 48.5 %all-to-all-start = ((bf16[128,16,128]{2,0,1:T(8,128)(2,1)}), bf16[128,16,128]{2,0,1:T(8,128)(2,1)S(1)}, u32[]{:S(2)}, u32[]{:S(2)}) async-start(bf16[128,16,128]{2,0,1:T(8,128)(2,1)} %copy.39), calls=%async_computation | async-start | bytes 1048576 | tf_op jit(solution)/shard_map/all_to_all | solution.py:201
Sparse Core Ops, SparseCore 0:
  10.2 47.7 all-gather.8
  61.1 39.6 all-reduce.4
  103.2 120.6 all-gather.10
  226.7 111.0 all-gather.6
  437.8 77.5 reduce-scatter.1
where the time goes:
time: 525 us; the launch traced here: 524 us
  blocking collectives  222 us (42%)
  waiting for transfers between devices  160 us (30%)
  matrix products  76.4 us (15%)
  other arithmetic  29.3 us (6%)
  between operations  16.7 us (3%)
  starting transfers between devices  11.8 us (2%)
  local copies, waits for them, and re-layouts  6.6 us (1%)
    psum x5, blocking collectives, tick(): value_grad = lax.psum(partial_grad, 'tensor').astype(jnp.bfloat16)  71.3 us
    dot_general x9, matrix products, transposed_product(): lax.dot_general(left, right, (((1,), (1,)), ((), ())), preferred_element_...  55.2 us
    psum x1, blocking collectives, shards(): lax.psum((jnp.sum(live_mask), jnp.sum(live_mask * returns)), 'dp')  41.5 us
    unnamed x1, blocking collectives  41.5 us
    ppermute x5, waiting for transfers between devices, passed_along(): lax.ppermute(value, axis, [(source, source + steps) for source in range(i...  40.1 us
    all_gather x1, waiting for transfers between devices, shards(): value_rows = lax.all_gather(value_weight[0], 'dp', axis=0, tiled=True)  38.7 us
    psum x1, blocking collectives, shards(): lax.psum(jnp.sum(live_mask * (returns - return_mean) ** 2), 'dp')  36.9 us
    all_gather x1, waiting for transfers between devices, shards(): out_cols = lax.all_gather(out_weight[0], 'dp', axis=1, tiled=True)  36.8 us
  transfers between devices with their start and end apart: 11, of which 9 were waited for; matrix products, arithmetic and copies ran while one was open for 20% of the time, Pallas kernels for 0%

commit v1 on v0

v1 whole, which is shorter than its diff:
```python
import jax
import jax.numpy as jnp
from jax import lax
from jax.experimental import pallas as pl
from jax.experimental.pallas import tpu as pltpu
from jax.sharding import PartitionSpec as P

D = 8192
HD = 128
KVH = 4
EPS = 1e-05
F32 = jnp.float32
BF16 = jnp.bfloat16
MESH = pl.DeviceIdType.MESH
COPIES = 200
ORDER = "mwmammammwamwgmbmgmwbmgbmgmgbmgbmggmmmmmmm"


def attention_weights(logits, length_row):
    span_len = logits.shape[-1]
    query_place = lax.broadcasted_iota(jnp.int32, (span_len, span_len), 0)
    key_place = lax.broadcasted_iota(jnp.int32, (span_len, span_len), 1)
    allowed = (key_place <= query_place)[None, None] & (
        key_place[None, None] < length_row[:, None, None, None]
    )
    masked = jnp.where(allowed, logits.astype(F32), -1e30)
    row_top = jnp.max(masked, axis=-1, keepdims=True)
    exponent = jnp.where(allowed, jnp.exp(masked - row_top), 0.0)
    return (exponent / jnp.sum(exponent, axis=-1, keepdims=True)).astype(BF16)


def dot(left, right):
    return jnp.dot(left, right, preferred_element_type=F32)


def split_pair(value):
    high = value.astype(BF16)
    return high, (value - high.astype(F32)).astype(BF16)


def kernel(
    att_ref, x_ref, gain_ref, wv_ref, w_ref, head_ref,
    go_ref, gv_ref, gg_ref,
    att_all, v_all, xf, part, sum1, r0, r1, r2, r2x, gr_all,
    sq, sq_in, bm, att_t, v_bd, up_bd, wb, wq, wvb, wvt, gains, rms_own, rms_all, hid, st, st_in,
    coef, ret, err_at, up, ng, vg, v_t, nrm_t, go_own, go_send, go_in, gv_own, gv_send, gv_in,
    gg_own, gg_send, gg_in,
    send_sems, recv_sems, local_sems,
):
    pipe = lax.axis_index("pipe")
    tensor = lax.axis_index("tensor")
    dp = lax.axis_index("dp")
    c = lax.rem(tensor, 2)
    xh = lax.div(tensor, 2)
    z = lax.div(dp, 4)
    y = lax.rem(dp, 4)
    a = jnp.where(c == 0, z, y)
    b = jnp.where(c == 0, y, z)
    other = 1 - pipe

    def dp_of(a_at, b_at):
        return jnp.where(c == 0, a_at * 4 + b_at, b_at * 4 + a_at)

    core_peer = {"tensor": xh * 2 + 1 - c}
    x_tensor = (1 - xh) * 2 + c
    x_peer = {"tensor": x_tensor}
    pipe_peer = {"pipe": other}
    a_next = [lax.rem(a + k, 4) for k in (1, 2, 3)]
    b_next = [lax.rem(b + k, 4) for k in (1, 2, 3)]
    a_peers = [{"dp": dp_of(at, b)} for at in a_next]
    ax_peers = [{"dp": dp_of(at, b), "tensor": x_tensor} for at in [a] + a_next]
    b_peers = [{"dp": dp_of(a, bt)} for bt in b_next]
    t_peers = [{"tensor": lax.rem(tensor + k, 4)} for k in (1, 2, 3)]
    dp_next = [lax.rem(dp + k, 16) for k in range(16)]
    used = [0]

    def remote(src, dst, device):
        at = used[0]
        used[0] += 1
        return pltpu.make_async_remote_copy(
            src_ref=src, dst_ref=dst, send_sem=send_sems.at[at], recv_sem=recv_sems.at[at],
            device_id=device, device_id_type=MESH,
        )

    def start(copies):
        for one in copies:
            one.start()
        return copies

    def finish(copies):
        for one in copies:
            one.wait()

    def rows_of(first, size):
        return pl.ds(pl.multiple_of(first, size), size)

    loads = [
        pltpu.make_async_copy(wv_ref, wvb.at[pipe], local_sems.at[0]),
        pltpu.make_async_copy(w_ref, wb.at[pipe], local_sems.at[1]),
    ]
    start(loads)
    barrier = pltpu.get_barrier_semaphore()
    partners = [{"dp": to} for to in dp_next[1:]] + t_peers + ax_peers[1:]
    partners += [{"dp": to, "pipe": other} for to in dp_next]
    partners += [{"tensor": one["tensor"], "pipe": other} for one in t_peers]
    for peer in partners:
        pl.semaphore_signal(barrier, inc=1, device_id=peer, device_id_type=MESH)
    pl.semaphore_wait(barrier, len(partners))

    def x_copy(to, device, half):
        return remote(
            x_ref.at[rows_of(half * 64, 64), rows_of(to * 128, 128)],
            xf.at[pipe, rows_of(dp * 64, 64)], device,
        )

    x_same = [x_copy(to, {"dp": to}, pipe) for to in dp_next[1:]]
    x_cross = [x_copy(to, {"dp": to, "pipe": other}, other) for to in dp_next]

    def send_x(layer):
        @pl.when(pipe == layer)
        def _():
            start(x_cross)
            start(x_same)
            xf[layer, rows_of(dp * 64, 64), :] = x_ref[rows_of(layer * 64, 64), rows_of(dp * 128, 128)]

    def wait_x(layer):
        @pl.when(pipe == layer)
        def _():
            finish(x_same)
            for one in x_cross:
                one.wait_send()

        @pl.when(pipe != layer)
        def _():
            for one in x_cross:
                one.wait_recv()

    att_cross = remote(att_ref.at[other], att_all.at[pipe, c, a, b, xh], pipe_peer)

    def gather_attention(layer):
        here = att_all.at[layer]

        @pl.when(pipe != layer)
        def _():
            att_cross.wait_recv()

        copies = start([remote(here.at[c, a, b, xh], here.at[c, a, b, xh], x_peer)])
        yield
        finish(copies)
        copies = start([remote(here.at[c, a, b], here.at[c, a, b], peer) for peer in a_peers])
        yield
        finish(copies)
        copies = start([remote(here.at[c, :, b], here.at[c, :, b], peer) for peer in b_peers])
        yield
        finish(copies)
        copies = start([remote(here.at[c], here.at[c], core_peer)])
        yield
        finish(copies)
        yield

    def scatter(layer, turn):
        here = part.at[turn]
        copies = start([remote(here.at[1 - c], r0.at[turn], core_peer)])
        yield
        finish(copies)

        def add0(at, carry):
            for bt in range(4):
                part[turn, c, at, bt] = (
                    part[turn, c, at, bt].astype(F32) + r0[turn, at, bt].astype(F32)
                ).astype(BF16)
            return carry

        lax.fori_loop(0, 4, add0, 0)
        copies = start([
            remote(here.at[c, :, bt], r1.at[turn, k], peer)
            for k, (bt, peer) in enumerate(zip(b_next, b_peers))
        ])
        yield
        finish(copies)
        for at in range(4):
            sum1[turn, at] = (
                part[turn, c, at, b].astype(F32) + r1[turn, 0, at].astype(F32)
                + r1[turn, 1, at].astype(F32) + r1[turn, 2, at].astype(F32)
            ).astype(BF16)
        copies = [
            remote(sum1.at[turn, at], r2x.at[turn, k], peer)
            for k, (at, peer) in enumerate(zip([a] + a_next, ax_peers))
        ]
        copies += [
            remote(sum1.at[turn, at], r2.at[turn, k], peer)
            for k, (at, peer) in enumerate(zip(a_next, a_peers))
        ]
        start(copies)
        yield
        finish(copies)

    def scattered(turn):
        total = sum1[turn, a].astype(F32)
        for k in range(3):
            total = total + r2[turn, k].astype(F32)
        for k in range(4):
            total = total + r2x[turn, k].astype(F32)
        return total

    def gather(here):
        copies = start([remote(here.at[c, a, b], here.at[c, a, b], peer) for peer in a_peers])
        yield
        finish(copies)
        copies = start([remote(here.at[c, :, b], here.at[c, :, b], peer) for peer in b_peers])
        yield
        finish(copies)
        copies = start([remote(here.at[c], here.at[c], core_peer)])
        yield
        finish(copies)

    head_row = head_ref[pl.ds(dp, 1), :]
    lane = lax.broadcasted_iota(jnp.int32, (128, 128), 1)

    def project(layer):
        gain_row = gains[layer, 0:1, :]

        def body(zi, carry):
            xg = (xf[layer, rows_of(zi * 256, 256), :].astype(F32) * gain_row).astype(BF16)
            out = dot(xg, wvb[layer]).astype(BF16)
            for yi in range(4):
                part[layer, 0, zi, yi] = out[yi * 64:yi * 64 + 32]
                part[layer, 1, yi, zi] = out[yi * 64 + 32:yi * 64 + 64]
            return carry

        lax.fori_loop(0, 4, body, 0)

    def forward(layer):
        wait_x(layer)
        project(layer)
        yield from scatter(layer, layer)
        rms = rms_own[layer, :, 0:1]
        total = scattered(layer) * rms
        high, low = split_pair(rms)
        place = lax.broadcasted_iota(jnp.int32, (32, 128), 1)
        extra = jnp.where(place == 0, high.astype(F32), jnp.where(place == 1, low.astype(F32), 0.0))
        v_all[layer, c, a, b, :, 0:512] = total.astype(BF16)
        v_all[layer, c, a, b, :, 512:640] = extra.astype(BF16)
        yield from gather(v_all.at[layer])

    def mixture():
        def body(zi, carry):
            for yi in range(4):
                first = pl.multiple_of(zi * 256 + yi * 64, 64)
                for g in range(4):
                    places = (0, zi, yi) if g % 2 == 0 else (1, yi, zi)
                    att = att_all[(1, *places, g // 2)][0:128, :]
                    cols = slice(g * 128, (g + 1) * 128)
                    for m in range(2):
                        values = v_all[(1, 0, zi, yi) if m == 0 else (1, 1, yi, zi)][:, cols]
                        for q in range(2):
                            at = q * 2 + m
                            v_bd[yi, g, at * 32:(at + 1) * 32, at * 128:(at + 1) * 128] = values
                    out = dot(att, v_bd[yi, g]).astype(BF16)
                    for h in range(4):
                        for q in range(2):
                            for m in range(2):
                                head = g * 8 + q * 4 + h
                                bm[1, pl.ds(first + m * 32, 32), head * 128:(head + 1) * 128] = (
                                    out[h * 32:(h + 1) * 32, (q * 2 + m) * 128:(q * 2 + m + 1) * 128]
                                )
            return carry

        lax.fori_loop(0, 4, body, 0)

    def out_project():
        def body(k, carry):
            rows = rows_of(k * 512, 512)
            hid[rows, :] = xf[1, rows, :].astype(F32) + dot(bm[1, rows, :], wb[1])
            return carry

        lax.fori_loop(0, 2, body, 0)
        tile = jnp.zeros((128, 128), F32)
        for k in range(8):
            h = hid[k * 128:(k + 1) * 128, :]
            tile = jnp.where(lane == k, jnp.sum(h * h, axis=1, keepdims=True), tile)
            tile = jnp.where(lane == 8 + k, jnp.sum(h * head_row, axis=1, keepdims=True), tile)
        st[0] = tile.T[0:16]

    def targets():
        for d in range(16):
            extra = att_all[1, 0, d // 4, d % 4, 0, 128:144, :].astype(F32)
            at = 8 * (d % 2) + d // 2
            ret[at:at + 1, :] = extra[0:1] + extra[1:2] + extra[2:3]
            ret[16 + at:17 + at, :] = extra[3:4]
        returns = ret[0:16, :]
        live = ret[16:32, :]

        def whole(value):
            return jnp.sum(jnp.sum(value, axis=1, keepdims=True), axis=0, keepdims=True)

        count = jnp.maximum(whole(live), 1.0)
        mean = whole(live * returns) / count
        spread = whole(live * (returns - mean) * (returns - mean)) / count
        target = (returns - mean) * lax.rsqrt(spread + EPS)
        low = lax.broadcasted_iota(jnp.int32, (8, 128), 1) < 64
        for at, value in enumerate((target, live)):
            even, odd = value[0:8], value[8:16]
            err_at[0, at] = jnp.where(low, even, pltpu.roll(odd, 64, 1))
            err_at[1, at] = jnp.where(low, pltpu.roll(even, 64, 1), odd)

    def upstream(sums):
        target, live = err_at[pipe, 0], err_at[pipe, 1]
        out_scale = lax.rsqrt(sums[0:8] / D + EPS)
        critic = out_scale * sums[8:16]
        alpha = live * (critic - target) * out_scale
        beta = alpha * out_scale * critic / D
        coef[...] = jnp.concatenate([alpha, beta, jnp.zeros((112, 128), F32)], axis=0).T
        for k in range(8):
            rows = slice(k * 128, (k + 1) * 128)
            up[1, rows, :] = (
                coef[:, k:k + 1] * head_row - coef[:, 8 + k:9 + k] * hid[rows, :]
            ).astype(BF16)

    def turn_attention(layer):
        def body(zi, carry):
            for yi in range(4):
                for g in range(4):
                    places = (0, zi, yi) if g % 2 == 0 else (1, yi, zi)
                    turned = att_all[(layer, *places, g // 2)][0:128, :].T
                    for q in range(2):
                        for m in range(2):
                            att_t[layer, zi * 4 + yi, m, (g * 2 + q) * 32:(g * 2 + q + 1) * 32, :] = (
                                turned[(q * 2 + m) * 32:(q * 2 + m + 1) * 32]
                            )
            return carry

        lax.fori_loop(0, 4, body, 0)

    def prepare(layer):
        gain_row = gains[layer, 0:1, :]

        def body(zi, carry):
            for pair in range(2):
                first = pl.multiple_of(zi * 256 + pair * 128, 128)
                packets = []
                for yi in (pair * 2, pair * 2 + 1):
                    packets.append(v_all.at[layer, 0, zi, yi])
                    packets.append(v_all.at[layer, 1, yi, zi])
                extra = jnp.concatenate([one[:, 512:640] for one in packets], axis=0).astype(F32)
                rms = extra[:, 0:1] + extra[:, 1:2]
                rms_all[layer, pl.ds(first, 128), :] = jnp.broadcast_to(rms, (128, 128))
                normed = xf[layer, pl.ds(first, 128), :].astype(F32) * rms * gain_row
                nrm_t[layer, :, pl.ds(first, 128)] = normed.astype(BF16).T
                for g in range(4):
                    cols = slice(g * 128, (g + 1) * 128)
                    values = jnp.concatenate([one[:, cols] for one in packets], axis=0)
                    v_t[layer, g, :, pl.ds(first, 128)] = values.T
            return carry

        lax.fori_loop(0, 4, body, 0)

    def unmix(layer):
        def spread(d, carry):
            for m in range(2):
                first = pl.multiple_of(d * 64 + m * 32, 32)
                rows = up[layer, pl.ds(first, 32), :]
                for h in range(4):
                    up_bd[m, h * 32:(h + 1) * 32, h * 128:(h + 1) * 128] = rows
                out = dot(att_t[layer, d, m], up_bd[m]).astype(BF16)
                for q in range(8):
                    bm[layer, pl.ds(first, 32), q * 512:(q + 1) * 512] = out[q * 32:(q + 1) * 32, :]
            return carry

        lax.fori_loop(0, 16, spread, 0)

        def body(k, carry):
            rows = rows_of(k * 512, 512)
            for g in range(4):
                cols = slice(g * 1024, (g + 1) * 1024)
                out = dot(bm[layer, rows, cols], wq[layer, cols, :]).astype(BF16)
                for zi in range(2):
                    for yi in range(4):
                        first = zi * 256 + yi * 64
                        into = slice(g * 128, (g + 1) * 128)
                        part[2 + layer, 0, k * 2 + zi, yi, :, into] = out[first:first + 32]
                        part[2 + layer, 1, yi, k * 2 + zi, :, into] = out[first + 32:first + 64]
            return carry

        lax.fori_loop(0, 2, body, 0)

    def norm_back(layer):
        def body(zi, carry):
            first = pl.multiple_of(zi * 256, 256)
            for yi in range(4):
                vg[layer, pl.ds(first + yi * 64, 32), :] = gr_all[layer, 0, zi, yi]
                vg[layer, pl.ds(first + yi * 64 + 32, 32), :] = gr_all[layer, 1, yi, zi]
            ng[layer, pl.ds(first, 256), :] = dot(vg[layer, pl.ds(first, 256), :], wvt[layer])
            return carry

        lax.fori_loop(0, 4, body, 0)

    def input_grad(layer):
        gain_row = gains[layer, 0:1, :]

        def body(zi, carry):
            for yi in range(4):
                for m in range(2):
                    rows = pl.ds(pl.multiple_of(zi * 256 + yi * 64 + m * 32, 32), 32)
                    values = v_all[(layer, 0, zi, yi) if m == 0 else (layer, 1, yi, zi)][:, 0:512]
                    product = vg[layer, rows, :].astype(F32) * values.astype(F32)
                    inner = jnp.sum(product, axis=1, keepdims=True)
                    rms = rms_all[layer, rows, :]
                    up[layer - 1, rows, :] = (
                        up[layer, rows, :].astype(F32) + rms * gain_row * ng[layer, rows, :]
                        - (rms * rms * (inner / D)) * xf[layer, rows, :].astype(F32)
                    ).astype(BF16)
            return carry

        lax.fori_loop(0, 4, body, 0)

    go_copies = [
        remote(go_send.at[k * 1024:(k + 1) * 1024], go_in.at[k * 1024:(k + 1) * 1024], pipe_peer)
        for k in range(4)
    ]
    gv_copy = remote(gv_send, gv_in, pipe_peer)
    gg_copy = remote(gg_send, gg_in, pipe_peer)

    def out_grad(layer):
        for g in range(4):
            def body(k, carry):
                out = dot(v_t[layer, g], bm[layer, :, rows_of(g * 1024 + k * 512, 512)])

                @pl.when(pipe == layer)
                def _():
                    for h in range(4):
                        go_own[rows_of(g * 1024 + k * 512 + h * 128, 128), :] = (
                            out[:, h * 128:(h + 1) * 128]
                        )

                @pl.when(pipe != layer)
                def _():
                    for h in range(4):
                        go_send[rows_of(g * 1024 + k * 512 + h * 128, 128), :] = (
                            out[:, h * 128:(h + 1) * 128].astype(BF16)
                        )

                return carry

            lax.fori_loop(0, 2, body, 0)

            @pl.when(pipe != layer)
            def _():
                go_copies[g].start()

    def small_grads(layer):
        def value_grad(k, total):
            cols = rows_of(k * 256, 256)
            return total + dot(nrm_t[layer, :, cols], vg[layer, cols, :])

        value_total = lax.fori_loop(0, 4, value_grad, jnp.zeros((128, 512), F32))

        def gain_grad(k, total):
            rows = rows_of(k * 128, 128)
            gained = ng[layer, rows, :] * xf[layer, rows, :].astype(F32) * rms_all[layer, rows, :]
            return total + jnp.sum(gained.reshape(16, 8, 128), axis=0)

        gain_total = lax.fori_loop(0, 8, gain_grad, jnp.zeros((8, 128), F32))

        @pl.when(pipe == layer)
        def _():
            gv_own[...] = value_total
            gg_own[...] = gain_total

        @pl.when(pipe != layer)
        def _():
            gv_send[...] = value_total.astype(BF16)
            gg_send[...] = gain_total
            gv_copy.start()
            gg_copy.start()

    def sum_up(copies, peers, at):
        for one in copies:
            one.wait()
        st[at + 1] = st[at] + st_in[at, 0] + st_in[at, 1] + st_in[at, 2]

    def main():
        yield from forward(1)
        mixture()
        out_project()
        copies = start([remote(st.at[0], st_in.at[0, k], peer) for k, peer in enumerate(t_peers)])
        yield
        turn_attention(1)
        targets()
        sum_up(copies, t_peers, 0)
        copies = start([remote(st.at[1], st_in.at[1, k], peer) for k, peer in enumerate(b_peers)])
        yield
        prepare(1)
        sum_up(copies, b_peers, 1)
        copies = start([remote(st.at[2], st_in.at[2, k], peer) for k, peer in enumerate(a_peers)])
        yield
        sum_up(copies, a_peers, 2)
        upstream(st[3])
        for layer in (1, 0):
            unmix(layer)
            turn = 2 + layer
            steps = scatter(layer, turn)
            next(steps)
            yield
            next(steps)
            out_grad(layer)
            yield
            yield from steps
            gr_all[layer, c, a, b] = scattered(turn).astype(BF16)
            steps = gather(gr_all.at[layer])
            next(steps)
            yield
            next(steps)
            if layer == 0:
                small_grads(1)
            yield
            yield from steps
            norm_back(layer)
            if layer == 1:
                input_grad(1)
        small_grads(0)
        yield

    def background():
        yield from forward(0)
        turn_attention(0)
        yield
        prepare(0)
        yield

    gains[pipe, 0:8, :] = jnp.broadcast_to(gain_ref[pl.ds(dp, 1), :], (8, 128))
    loads[0].wait()
    cross = [
        remote(gains.at[pipe], gains.at[pipe], pipe_peer),
        remote(wvb.at[pipe], wvb.at[pipe], pipe_peer),
    ]
    send_x(1)
    start(cross)
    att_cross.start()
    att_all[pipe, c, a, b, xh] = att_ref[pipe]
    for m in range(4):
        rows = x_ref[m * 32:(m + 1) * 32, :].astype(F32)
        sq[m] = jnp.broadcast_to(jnp.sum(rows * rows, axis=1, keepdims=True), (32, 128))
    sq_in[pipe, tensor] = sq[pipe * 2 + c]
    squares = []
    for peer in t_peers:
        own = lax.rem(peer["tensor"], 2)
        squares.append(remote(sq.at[pipe * 2 + own], sq_in.at[pipe, tensor], peer))
        squares.append(remote(
            sq.at[other * 2 + own], sq_in.at[pipe, tensor], {"tensor": peer["tensor"], "pipe": other}
        ))
    squares.append(remote(sq.at[other * 2 + c], sq_in.at[pipe, tensor], pipe_peer))
    start(squares)
    attention1 = gather_attention(1)
    next(attention1)
    loads[1].wait()

    def turn_w(layer):
        def body(k, carry):
            wq[layer, rows_of(k * 128, 128), :] = wb[layer, rows_of(k * 128, 128), :].T
            return carry

        lax.fori_loop(0, 32, body, 0)
        for k in range(4):
            wvt[layer, k * 128:(k + 1) * 128, :] = wvb[layer, :, k * 128:(k + 1) * 128].T

    v_bd[...] = jnp.zeros_like(v_bd)
    up_bd[...] = jnp.zeros_like(up_bd)
    finish(squares)
    for layer in range(2):
        squared = sq_in[layer, 0] + sq_in[layer, 1] + sq_in[layer, 2] + sq_in[layer, 3]
        rms_own[layer] = lax.rsqrt(squared / D + EPS)
    finish(cross)
    next(attention1)

    @pl.when(pipe == 1)
    def _():
        att_cross.wait_send()

    w_cross = remote(wb.at[pipe], wb.at[pipe], pipe_peer)

    def weights():
        w_cross.start()
        send_x(0)
        yield
        w_cross.wait()
        yield
        turn_w(1)
        yield
        turn_w(0)
        yield

    streams = {
        "m": main(), "g": background(), "a": attention1, "b": gather_attention(0), "w": weights(),
    }
    for name in ORDER:
        next(streams[name])

    @pl.when(pipe == 0)
    def _():
        att_cross.wait_send()

    def add_halves(k, carry):
        rows = rows_of(k * 256, 256)
        go_ref[rows, :] = (go_own[rows, :] + go_in[rows, :].astype(F32)).astype(BF16)
        return carry

    for one in go_copies:
        one.wait()
    lax.fori_loop(0, 16, add_halves, 0)
    gv_copy.wait()
    gg_copy.wait()
    gv_ref[...] = (gv_own[...] + gv_in[...].astype(F32)).astype(BF16)
    gg_ref[...] = jnp.sum(gg_own[...] + gg_in[...], axis=0, keepdims=True)


def shards(
    layer_inputs, norm_gain, value_weight, out_weight, scores, head_weight, lengths, returns,
    response_mask,
):
    replica = lax.axis_index("dp")
    own_lengths = lax.dynamic_index_in_dim(lengths, replica, 0, keepdims=False)
    attention = attention_weights(scores[0, 0], own_lengths)
    packed = attention.reshape(2, 2, 2, 4, 32, 32).transpose(0, 3, 4, 2, 1, 5).reshape(2, 128, 128)
    position = jnp.arange(128, dtype=jnp.int32)
    block_len = jnp.repeat(own_lengths, 32, total_repeat_length=128)
    live = ((position % 32 < block_len) & (response_mask == 1)).astype(F32)
    high = returns.astype(BF16)
    rest = returns - high.astype(F32)
    middle = rest.astype(BF16)
    low = (rest - middle.astype(F32)).astype(BF16)
    extra = jnp.stack([high, middle, low, live.astype(BF16)])
    extra = jnp.concatenate([extra, jnp.zeros((12, 128), BF16)], axis=0)
    packet = jnp.concatenate([packed, jnp.broadcast_to(extra, (2, 16, 128))], axis=1)

    vmem = pl.BlockSpec(memory_space=pltpu.VMEM)
    anywhere = pl.BlockSpec(memory_space=pl.ANY)

    def scratch(*shape, dtype=BF16):
        return pltpu.VMEM(shape, dtype)

    grad_out, grad_value, grad_gain = pl.pallas_call(
        kernel,
        out_shape=(
            jax.ShapeDtypeStruct((4096, 128), BF16),
            jax.ShapeDtypeStruct((128, 512), BF16),
            jax.ShapeDtypeStruct((1, 128), F32),
        ),
        in_specs=[vmem, vmem, vmem, anywhere, anywhere, vmem],
        out_specs=(vmem, vmem, vmem),
        scratch_shapes=[
            scratch(2, 2, 4, 4, 2, 144, 128),
            scratch(2, 2, 4, 4, 32, 640),
            scratch(2, 1024, 128),
            scratch(4, 2, 4, 4, 32, 512),
            scratch(4, 4, 32, 512),
            scratch(4, 4, 4, 32, 512),
            scratch(4, 3, 4, 32, 512),
            scratch(4, 3, 32, 512),
            scratch(4, 4, 32, 512),
            scratch(2, 2, 4, 4, 32, 512),
            scratch(4, 32, 128, dtype=F32),
            scratch(2, 4, 32, 128, dtype=F32),
            scratch(2, 1024, 4096),
            scratch(2, 16, 2, 256, 128),
            scratch(4, 4, 128, 512),
            scratch(2, 128, 512),
            scratch(2, 4096, 128),
            scratch(2, 4096, 128),
            scratch(2, 128, 512),
            scratch(2, 512, 128),
            scratch(2, 8, 128, dtype=F32),
            scratch(2, 32, 128, dtype=F32),
            scratch(2, 1024, 128, dtype=F32),
            scratch(1024, 128, dtype=F32),
            scratch(4, 16, 128, dtype=F32),
            scratch(3, 3, 16, 128, dtype=F32),
            scratch(128, 128, dtype=F32),
            scratch(32, 128, dtype=F32),
            scratch(2, 2, 8, 128, dtype=F32),
            scratch(2, 1024, 128),
            scratch(2, 1024, 128, dtype=F32),
            scratch(2, 1024, 512),
            scratch(2, 4, 128, 1024),
            scratch(2, 128, 1024),
            scratch(4096, 128, dtype=F32),
            scratch(4096, 128),
            scratch(4096, 128),
            scratch(128, 512, dtype=F32),
            scratch(128, 512),
            scratch(128, 512),
            scratch(8, 128, dtype=F32),
            scratch(8, 128, dtype=F32),
            scratch(8, 128, dtype=F32),
            pltpu.SemaphoreType.DMA((COPIES,)),
            pltpu.SemaphoreType.DMA((COPIES,)),
            pltpu.SemaphoreType.DMA((2,)),
        ],
        compiler_params=pltpu.CompilerParams(
            collective_id=0, has_side_effects=True, vmem_limit_bytes=60 * 1024 * 1024
        ),
        cost_estimate=pl.CostEstimate(
            flops=8_000_000_000, bytes_accessed=6_000_000, transcendentals=0
        ),
    )(
        packet,
        layer_inputs[0],
        norm_gain[0].reshape(16, 128),
        value_weight[0],
        out_weight[0],
        head_weight.astype(F32).reshape(16, 128),
    )
    return grad_out[None], grad_value[None], grad_gain


def solution(mesh):
    return jax.shard_map(
        shards,
        mesh=mesh,
        in_specs=(
            P("pipe", "dp", "tensor"),
            P("pipe", "tensor"),
            P("pipe", ("tensor", "dp"), None),
            P("pipe", None, ("tensor", "dp")),
            P("pipe", "dp", None, "tensor", None, None),
            P("tensor"),
            P(),
            P("dp"),
            P("dp"),
        ),
        out_specs=(
            P("pipe", None, ("tensor", "dp")),
            P("pipe", ("tensor", "dp"), None),
            P("pipe", ("tensor", "dp")),
        ),
        check_vma=False,
    )
```

time: 525 us -> 205 us (0.39)
  blocking collectives: 222 us -> 0 us
  Pallas kernels: 0 us -> 187 us
  waiting for transfers between devices: 160 us -> 0 us
  matrix products: 76.4 us -> 0 us
  other arithmetic: 29.3 us -> 9.16 us
  between operations: 16.7 us -> 0.76 us
  starting transfers between devices: 11.8 us -> 0 us
    pallas_call x0 -> x1, Pallas kernels: none -> 187 us  [shards(): pl.pallas_call(kernel, out_shape=(jax.ShapeDtypeStruct((4096, 128), BF16)...]
    psum x9 -> x0, blocking collectives: 169 us -> none  [the longest x5 71.3 us: tick(): value_grad = lax.psum(partial_grad, 'tensor').astype(jnp.bfloat16)]
    dot_general x17 -> x0, matrix products: 76.4 us -> none  [the longest x9 55.2 us: transposed_product(): lax.dot_general(left, right, (((1,), (1,)), ((), ())), preferred_element_...]
    all_gather x3 -> x0, waiting for transfers between devices: 75.5 us -> none  [the longest x1 38.7 us: shards(): value_rows = lax.all_gather(value_weight[0], 'dp', axis=0, tiled=True)]
    unnamed x1 -> x0, blocking collectives: 41.5 us -> none
    ppermute x5 -> x0, waiting for transfers between devices: 40.1 us -> none  [passed_along(): lax.ppermute(value, axis, [(source, source + steps) for source in range(i...]
    psum x1 -> x0, waiting for transfers between devices: 24.3 us -> none  [shards(): lax.psum(jnp.dot(normed, value_rows, preferred_element_type=jnp.float32),...]
    reduce_scatter x1 -> x0, waiting for transfers between devices: 18.8 us -> none  [shards(): lax.psum_scatter(weight_part, 'dp', scatter_dimension=0, tiled=True)]
  transfers between devices with their start and end apart: 11 -> 0, of which waited for: 9 -> 0; matrix products, arithmetic and copies ran while one was open for 20% -> 0% of each run, Pallas kernels for 0% -> 0%
where the time goes in v1:
time: 205 us; the launch traced here: 203 us
  Pallas kernels  187 us (91%)
  other arithmetic  9.16 us (4%)
  local copies, waits for them, and re-layouts  5.73 us (3%)
    pallas_call x1, Pallas kernels, shards(): pl.pallas_call(kernel, out_shape=(jax.ShapeDtypeStruct((4096, 128), BF16)...  187 us

profile of v1, /device:TPU:0, one launch (start us, length us, event | category | flops | bytes accessed | tf_op | source)
XLA Modules:
  0.0 203.0 jit_solution(3582631426868189689)
XLA Ops:
  0.6 0.0 copy-start.2
  0.6 0.0 copy-start.3
  0.7 0.0 copy-start.4
  0.7 0.0 copy-start
  0.7 0.7 convert_bitcast_fusion.1
  1.4 0.9 fusion.8
  2.3 0.6 fusion.9
  2.8 0.0 copy-done.2
  2.8 0.0 copy-done.3
  2.8 0.0 copy-done.4
  2.9 3.2 %convert_bitcast_fusion = bf16[1,128]{1,0:T(2,128)(2,1)S(1)} fusion(s32[128]{0:T(128)} %param.19, pred[128]{0:T(512)(128)(4,1)S(1)} %copy-done.4, pred[128]{0:T(512)(128)(4,1)S(1)} %copy-done.3, pred[128]{0:T(512)(128)(4,1)S(1)} %copy-done.2, s32[]{:T(128)} %bitcast.11, s32[]{:T(128)} %bitcast.8, s32[]{:T(128)} %bitcast.9, s32[]{:T(128)} %bitcast.10), kind=kLoop, calls=%fused_computation.18 | loop fusion | flops 1792 | bytes 1168 | tf_op jit(solution)/shard_map/stack | solution.py:632
  6.1 0.1 lt.53
  6.2 0.1 concatenate.10
  6.3 1.3 bitcast_convert_fusion.head_ref
  7.6 0.1 fusion.7
  7.7 1.2 fusion.5
  8.9 0.0 copy-done
  8.9 0.4 select_reduce_fusion
  9.3 0.1 compare_and_fusion
  9.4 0.2 copy.15
  9.6 0.2 copy.16
  9.9 1.5 fusion.6
  11.3 0.2 reshape.88
  11.5 0.6 pad_maximum_fusion.att_ref
  12.2 187.4 %shard_map.112 = (bf16[4096,128]{1,0:T(8,128)(2,1)}, bf16[128,512]{1,0:T(8,128)(2,1)}, f32[1,128]{1,0:T(1,128)}) custom-call(bf16[2,144,128]{2,1,0:T(8,128)(2,1)} %pad_maximum_fusion.att_ref, bf16[128,2048]{1,0:T(8,128)(2,1)} %bitcast.39, f32[16,128]{1,0:T(8,128)} %bitcast.41, bf16[128,512]{1,0:T(8,128)(2,1)} %bitcast.40, bf16[4096,128]{1,0:T(8,128)(2,1)} %bitcast.38, ...), custom_call_target="tpu_custom_call" | custom-call | flops 8000000000 | bytes 6000000 | tf_op jit(solution)/shard_map/pallas_call | solution.py:642
  199.6 0.0 copy-start.1
  199.6 2.3 %copy.33 = bf16[1,4096,128]{2,1,0:T(8,128)(2,1)} copy(bf16[1,4096,128]{2,1,0:T(8,128)(2,1)} %bitcast.34) | data formatting | bytes 2097152
  201.9 0.0 copy-done.1
  201.9 0.0 copy-start.5
  201.9 0.7 copy.34
  202.5 0.0 copy-done.5
  202.5 0.5 copy.35
  (4 shorter events, 0.1 us)
Async XLA Ops:
  0.6 2.2 %copy-start.2 = (pred[128]{0:T(512)(128)(4,1)S(1)}, pred[128]{0:T(512)(128)(4,1)}, u32[]{:S(2)}) copy-start(pred[128]{0:T(512)(128)(4,1)} %constant.124) | copy-start | bytes 388
  0.6 2.2 %copy-start.3 = (pred[128]{0:T(512)(128)(4,1)S(1)}, pred[128]{0:T(512)(128)(4,1)}, u32[]{:S(2)}) copy-start(pred[128]{0:T(512)(128)(4,1)} %constant.123) | copy-start | bytes 388
  0.7 2.2 %copy-start.4 = (pred[128]{0:T(512)(128)(4,1)S(1)}, pred[128]{0:T(512)(128)(4,1)}, u32[]{:S(2)}) copy-start(pred[128]{0:T(512)(128)(4,1)} %constant.122) | copy-start | bytes 388
  0.7 8.2 %copy-start = (bf16[1,1,4,8,32,32]{5,4,3,2,1,0:T(8,128)(2,1)S(1)}, bf16[1,1,4,8,32,32]{5,4,3,2,1,0:T(8,128)(2,1)}, u32[]{:S(2)}) copy-start(bf16[1,1,4,8,32,32]{5,4,3,2,1,0:T(8,128)(2,1)} %param.15) | copy-start | bytes 196612
  199.6 2.3 %copy-start.1 = (bf16[128,512]{1,0:T(8,128)(2,1)S(1)}, bf16[128,512]{1,0:T(8,128)(2,1)}, u32[]{:S(2)}) copy-start(bf16[128,512]{1,0:T(8,128)(2,1)} %get-tuple-element.19) | copy-start | bytes 393220
  201.9 0.7 copy-start.5

commit v2 on v1

--- a/solution.py
+++ b/solution.py
@@ -13,7 +13,7 @@
 BF16 = jnp.bfloat16
 MESH = pl.DeviceIdType.MESH
 COPIES = 200
-ORDER = "mwmammammwamwgmbmgmwbmgbmgmgbmgbmggmmmmmmm"
+ORDER = "mwmawwmmawmwwmawsmwwmwmbuumuugmuubugmugmbgmubgmoogmbougmgoomooqqqmmoqmqqmqqm"
 
 
 def attention_weights(logits, length_row):
@@ -415,8 +415,8 @@
         lax.fori_loop(0, 4, body, 0)
 
     go_copies = [
-        remote(go_send.at[k * 1024:(k + 1) * 1024], go_in.at[k * 1024:(k + 1) * 1024], pipe_peer)
-        for k in range(4)
+        remote(go_send.at[k * 512:(k + 1) * 512], go_in.at[k * 512:(k + 1) * 512], pipe_peer)
+        for k in range(8)
     ]
     gv_copy = remote(gv_send, gv_in, pipe_peer)
     gg_copy = remote(gg_send, gg_in, pipe_peer)
@@ -444,10 +444,6 @@
 
             lax.fori_loop(0, 2, body, 0)
 
-            @pl.when(pipe != layer)
-            def _():
-                go_copies[g].start()
-
     def small_grads(layer):
         def value_grad(k, total):
             cols = rows_of(k * 256, 256)
@@ -482,6 +478,7 @@
     def main():
         yield from forward(1)
         mixture()
+        yield
         out_project()
         copies = start([remote(st.at[0], st_in.at[0, k], peer) for k, peer in enumerate(t_peers)])
         yield
@@ -577,21 +574,43 @@
     def _():
         att_cross.wait_send()
 
-    w_cross = remote(wb.at[pipe], wb.at[pipe], pipe_peer)
-
-    def weights():
-        w_cross.start()
+    w_copies = [
+        remote(wb.at[pipe, k * 512:(k + 1) * 512], wb.at[pipe, k * 512:(k + 1) * 512], pipe_peer)
+        for k in range(8)
+    ]
+
+    def pieces(copies, sender):
+        for one in copies:
+            @pl.when(pipe == sender)
+            def _():
+                one.start()
+
+            yield
+
+    def weights(layer):
+        for _ in pieces(w_copies, layer):
+            yield
+        for one in w_copies:
+            @pl.when(pipe == layer)
+            def _():
+                one.wait_send()
+
+            @pl.when(pipe != layer)
+            def _():
+                one.wait_recv()
+
+        yield
+        turn_w(layer)
+        yield
+
+    def send_other_x():
         send_x(0)
         yield
-        w_cross.wait()
-        yield
-        turn_w(1)
-        yield
-        turn_w(0)
-        yield
 
     streams = {
-        "m": main(), "g": background(), "a": attention1, "b": gather_attention(0), "w": weights(),
+        "m": main(), "g": background(), "a": attention1, "b": gather_attention(0),
+        "w": weights(1), "u": weights(0), "s": send_other_x(),
+        "o": pieces(go_copies, 0), "q": pieces(go_copies, 1),
     }
     for name in ORDER:
         next(streams[name])

time: 205 us -> 181 us (0.88)
  Pallas kernels: 187 us -> 165 us
    pallas_call x1, Pallas kernels: 187 us -> 165 us  [shards(): pl.pallas_call(kernel, out_shape=(jax.ShapeDtypeStruct((4096, 128), BF16)...]
where the time goes in v2:
time: 181 us
  Pallas kernels  165 us (91%)
  other arithmetic  9.16 us (5%)
  local copies, waits for them, and re-layouts  5.73 us (3%)
    pallas_call x1, Pallas kernels, shards(): pl.pallas_call(kernel, out_shape=(jax.ShapeDtypeStruct((4096, 128), BF16)...  165 us
    another operation x2, other arithmetic, shards(): extra = jnp.stack([high, middle, low, live.astype(BF16)])  3.97 us

profile of v2, /device:TPU:0, one launch (start us, length us, event | category | flops | bytes accessed | tf_op | source)
XLA Modules:
  0.0 180.9 jit_solution(9283746991394232072)
XLA Ops:
  0.6 0.0 copy-start.2
  0.6 0.0 copy-start.3
  0.7 0.0 copy-start.4
  0.7 0.0 copy-start
  0.7 0.7 convert_bitcast_fusion.1
  1.4 0.9 fusion.8
  2.3 0.6 fusion.9
  2.8 0.0 copy-done.2
  2.8 0.0 copy-done.3
  2.8 0.0 copy-done.4
  2.9 3.2 %convert_bitcast_fusion = bf16[1,128]{1,0:T(2,128)(2,1)S(1)} fusion(s32[128]{0:T(128)} %param.19, pred[128]{0:T(512)(128)(4,1)S(1)} %copy-done.4, pred[128]{0:T(512)(128)(4,1)S(1)} %copy-done.3, pred[128]{0:T(512)(128)(4,1)S(1)} %copy-done.2, s32[]{:T(128)} %bitcast.11, s32[]{:T(128)} %bitcast.8, s32[]{:T(128)} %bitcast.9, s32[]{:T(128)} %bitcast.10), kind=kLoop, calls=%fused_computation.18 | loop fusion | flops 1792 | bytes 1168 | tf_op jit(solution)/shard_map/stack | solution.py:651
  6.1 0.1 lt.53
  6.2 0.1 concatenate.10
  6.3 1.3 bitcast_convert_fusion.head_ref
  7.6 0.1 fusion.7
  7.7 1.2 fusion.5
  8.9 0.0 copy-done
  8.9 0.4 select_reduce_fusion
  9.3 0.1 compare_and_fusion
  9.4 0.2 copy.15
  9.6 0.2 copy.16
  9.9 1.5 fusion.6
  11.3 0.2 reshape.88
  11.5 0.6 pad_maximum_fusion.att_ref
  12.2 165.2 %shard_map.112 = (bf16[4096,128]{1,0:T(8,128)(2,1)}, bf16[128,512]{1,0:T(8,128)(2,1)}, f32[1,128]{1,0:T(1,128)}) custom-call(bf16[2,144,128]{2,1,0:T(8,128)(2,1)} %pad_maximum_fusion.att_ref, bf16[128,2048]{1,0:T(8,128)(2,1)} %bitcast.39, f32[16,128]{1,0:T(8,128)} %bitcast.41, bf16[128,512]{1,0:T(8,128)(2,1)} %bitcast.40, bf16[4096,128]{1,0:T(8,128)(2,1)} %bitcast.38, ...), custom_call_target="tpu_custom_call" | custom-call | flops 8000000000 | bytes 6000000 | tf_op jit(solution)/shard_map/pallas_call | solution.py:661
  177.4 0.0 copy-start.1
  177.4 2.3 %copy.33 = bf16[1,4096,128]{2,1,0:T(8,128)(2,1)} copy(bf16[1,4096,128]{2,1,0:T(8,128)(2,1)} %bitcast.34) | data formatting | bytes 2097152
  179.7 0.0 copy-done.1
  179.7 0.0 copy-start.5
  179.7 0.7 copy.34
  180.4 0.0 copy-done.5
  180.4 0.5 copy.35
  (4 shorter events, 0.1 us)
Async XLA Ops:
  0.6 2.2 %copy-start.2 = (pred[128]{0:T(512)(128)(4,1)S(1)}, pred[128]{0:T(512)(128)(4,1)}, u32[]{:S(2)}) copy-start(pred[128]{0:T(512)(128)(4,1)} %constant.124) | copy-start | bytes 388
  0.6 2.2 %copy-start.3 = (pred[128]{0:T(512)(128)(4,1)S(1)}, pred[128]{0:T(512)(128)(4,1)}, u32[]{:S(2)}) copy-start(pred[128]{0:T(512)(128)(4,1)} %constant.123) | copy-start | bytes 388
  0.7 2.2 %copy-start.4 = (pred[128]{0:T(512)(128)(4,1)S(1)}, pred[128]{0:T(512)(128)(4,1)}, u32[]{:S(2)}) copy-start(pred[128]{0:T(512)(128)(4,1)} %constant.122) | copy-start | bytes 388
  0.7 8.2 %copy-start = (bf16[1,1,4,8,32,32]{5,4,3,2,1,0:T(8,128)(2,1)S(1)}, bf16[1,1,4,8,32,32]{5,4,3,2,1,0:T(8,128)(2,1)}, u32[]{:S(2)}) copy-start(bf16[1,1,4,8,32,32]{5,4,3,2,1,0:T(8,128)(2,1)} %param.15) | copy-start | bytes 196612
  177.4 2.3 %copy-start.1 = (bf16[128,512]{1,0:T(8,128)(2,1)S(1)}, bf16[128,512]{1,0:T(8,128)(2,1)}, u32[]{:S(2)}) copy-start(bf16[128,512]{1,0:T(8,128)(2,1)} %get-tuple-element.19) | copy-start | bytes 393220
  179.7 0.7 copy-start.5

commit v3 on v2

--- a/solution.py
+++ b/solution.py
@@ -13,20 +13,31 @@
 BF16 = jnp.bfloat16
 MESH = pl.DeviceIdType.MESH
 COPIES = 200
-ORDER = "mwmawwmmawmwwmawsmwwmwmbuumuugmuubugmugmbgmubgmoogmbougmgoomooqqqmmoqmqqmqqm"
-
-
-def attention_weights(logits, length_row):
-    span_len = logits.shape[-1]
-    query_place = lax.broadcasted_iota(jnp.int32, (span_len, span_len), 0)
-    key_place = lax.broadcasted_iota(jnp.int32, (span_len, span_len), 1)
-    allowed = (key_place <= query_place)[None, None] & (
-        key_place[None, None] < length_row[:, None, None, None]
-    )
-    masked = jnp.where(allowed, logits.astype(F32), -1e30)
-    row_top = jnp.max(masked, axis=-1, keepdims=True)
-    exponent = jnp.where(allowed, jnp.exp(masked - row_top), 0.0)
-    return (exponent / jnp.sum(exponent, axis=-1, keepdims=True)).astype(BF16)
+ORDER = (
+    "mw",
+    "maww",
+    "m",
+    "maw",
+    "mww",
+    "maws",
+    "mww",
+    "mw",
+    "mbuu",
+    "muug",
+    "muubug",
+    "mug",
+    "mbg",
+    "mubg",
+    "moog",
+    "mboug",
+    "mgoo",
+    "mooqqq",
+    "m",
+    "moq",
+    "mqq",
+    "mqq",
+    "m",
+)
 
 
 def dot(left, right):
@@ -39,11 +50,11 @@
 
 
 def kernel(
-    att_ref, x_ref, gain_ref, wv_ref, w_ref, head_ref,
-    go_ref, gv_ref, gg_ref,
-    att_all, v_all, xf, part, sum1, r0, r1, r2, r2x, gr_all,
+    score_ref, length_ref, return_ref, mask_ref, x_ref, gain_ref, wv_ref, w_ref, head_ref,
+    go_own, go_in, gv_ref, gg_ref,
+    att_own, att_all, v_all, xf, part, sum1, r0, r1, r2, r2x, gr_all,
     sq, sq_in, bm, att_t, v_bd, up_bd, wb, wq, wvb, wvt, gains, rms_own, rms_all, hid, st, st_in,
-    coef, ret, err_at, up, ng, vg, v_t, nrm_t, go_own, go_send, go_in, gv_own, gv_send, gv_in,
+    coef, ret, err_at, up, ng, vg, v_t, nrm_t, go_keep, go_send, gv_own, gv_send, gv_in,
     gg_own, gg_send, gg_in,
     send_sems, recv_sems, local_sems,
 ):
@@ -135,7 +146,38 @@
             for one in x_cross:
                 one.wait_recv()
 
-    att_cross = remote(att_ref.at[other], att_all.at[pipe, c, a, b, xh], pipe_peer)
+    att_cross = remote(att_own.at[other], att_all.at[pipe, c, a, b, xh], pipe_peer)
+
+    def attend():
+        row = lax.rem(lax.broadcasted_iota(jnp.int32, (256, 32), 0), 32)
+        key = lax.broadcasted_iota(jnp.int32, (256, 32), 1)
+        span = [length_ref[m, dp] for m in range(4)]
+        weights = []
+        for m in range(4):
+            allowed = (key <= row) & (key < span[m])
+            masked = jnp.where(allowed, score_ref[m].astype(F32).reshape(256, 32), -1e30)
+            top = jnp.max(masked, axis=1, keepdims=True)
+            exponent = jnp.where(allowed, jnp.exp(masked - top), 0.0)
+            weights.append(exponent / jnp.sum(exponent, axis=1, keepdims=True))
+        position = lax.broadcasted_iota(jnp.int32, (1, 128), 1)
+        block = lax.div(position, 32)
+        length = jnp.where(block == 0, span[0], span[1])
+        length = jnp.where(block == 2, span[2], length)
+        length = jnp.where(block == 3, span[3], length)
+        live = ((lax.rem(position, 32) < length) & (mask_ref[...] == 1)).astype(F32)
+        returns = return_ref[...]
+        high = returns.astype(BF16).astype(F32)
+        middle = (returns - high).astype(BF16).astype(F32)
+        low = (returns - high - middle).astype(BF16).astype(F32)
+        at = lax.broadcasted_iota(jnp.int32, (16, 128), 0)
+        extra = jnp.where(at == 0, high, jnp.where(at == 1, middle, jnp.where(at == 2, low, 0.0)))
+        extra = jnp.where(at == 3, live, extra).astype(BF16)
+        for half in range(2):
+            tile = [
+                weights[half * 2 + m][q * 128:(q + 1) * 128] for q in range(2) for m in range(2)
+            ]
+            att_own[half, 0:128, :] = jnp.concatenate(tile, axis=1).astype(BF16)
+            att_own[half, 128:144, :] = extra
 
     def gather_attention(layer):
         here = att_all.at[layer]
@@ -159,15 +201,15 @@
         yield
 
     def scatter(layer, turn):
-        here = part.at[turn]
+        here = part.at[layer]
         copies = start([remote(here.at[1 - c], r0.at[turn], core_peer)])
         yield
         finish(copies)
 
         def add0(at, carry):
             for bt in range(4):
-                part[turn, c, at, bt] = (
-                    part[turn, c, at, bt].astype(F32) + r0[turn, at, bt].astype(F32)
+                part[layer, c, at, bt] = (
+                    part[layer, c, at, bt].astype(F32) + r0[turn, at, bt].astype(F32)
                 ).astype(BF16)
             return carry
 
@@ -180,7 +222,7 @@
         finish(copies)
         for at in range(4):
             sum1[turn, at] = (
-                part[turn, c, at, b].astype(F32) + r1[turn, 0, at].astype(F32)
+                part[layer, c, at, b].astype(F32) + r1[turn, 0, at].astype(F32)
                 + r1[turn, 1, at].astype(F32) + r1[turn, 2, at].astype(F32)
             ).astype(BF16)
         copies = [
@@ -214,7 +256,9 @@
         yield
         finish(copies)
 
-    head_row = head_ref[pl.ds(dp, 1), :]
+    heads = head_ref[...].astype(F32)
+    head_at = lax.broadcasted_iota(jnp.int32, (16, 128), 0)
+    head_row = jnp.sum(jnp.where(head_at == dp, heads, 0.0), axis=0, keepdims=True)
     lane = lax.broadcasted_iota(jnp.int32, (128, 128), 1)
 
     def project(layer):
@@ -378,8 +422,8 @@
                     for yi in range(4):
                         first = zi * 256 + yi * 64
                         into = slice(g * 128, (g + 1) * 128)
-                        part[2 + layer, 0, k * 2 + zi, yi, :, into] = out[first:first + 32]
-                        part[2 + layer, 1, yi, k * 2 + zi, :, into] = out[first + 32:first + 64]
+                        part[layer, 0, k * 2 + zi, yi, :, into] = out[first:first + 32]
+                        part[layer, 1, yi, k * 2 + zi, :, into] = out[first + 32:first + 64]
             return carry
 
         lax.fori_loop(0, 2, body, 0)
@@ -418,6 +462,7 @@
         remote(go_send.at[k * 512:(k + 1) * 512], go_in.at[k * 512:(k + 1) * 512], pipe_peer)
         for k in range(8)
     ]
+    keep = pltpu.make_async_copy(go_keep, go_own, local_sems.at[2])
     gv_copy = remote(gv_send, gv_in, pipe_peer)
     gg_copy = remote(gg_send, gg_in, pipe_peer)
 
@@ -429,8 +474,8 @@
                 @pl.when(pipe == layer)
                 def _():
                     for h in range(4):
-                        go_own[rows_of(g * 1024 + k * 512 + h * 128, 128), :] = (
-                            out[:, h * 128:(h + 1) * 128]
+                        go_keep[rows_of(g * 1024 + k * 512 + h * 128, 128), :] = (
+                            out[:, h * 128:(h + 1) * 128].astype(BF16)
                         )
 
                 @pl.when(pipe != layer)
@@ -443,6 +488,10 @@
                 return carry
 
             lax.fori_loop(0, 2, body, 0)
+
+        @pl.when(pipe == layer)
+        def _():
+            keep.start()
 
     def small_grads(layer):
         def value_grad(k, total):
@@ -525,7 +574,7 @@
         prepare(0)
         yield
 
-    gains[pipe, 0:8, :] = jnp.broadcast_to(gain_ref[pl.ds(dp, 1), :], (8, 128))
+    gains[pipe, 0:8, :] = jnp.broadcast_to(gain_ref[:, rows_of(dp * 128, 128)], (8, 128))
     loads[0].wait()
     cross = [
         remote(gains.at[pipe], gains.at[pipe], pipe_peer),
@@ -533,8 +582,9 @@
     ]
     send_x(1)
     start(cross)
+    attend()
     att_cross.start()
-    att_all[pipe, c, a, b, xh] = att_ref[pipe]
+    att_all[pipe, c, a, b, xh] = att_own[pipe]
     for m in range(4):
         rows = x_ref[m * 32:(m + 1) * 32, :].astype(F32)
         sq[m] = jnp.broadcast_to(jnp.sum(rows * rows, axis=1, keepdims=True), (32, 128))
@@ -612,66 +662,59 @@
         "w": weights(1), "u": weights(0), "s": send_other_x(),
         "o": pieces(go_copies, 0), "q": pieces(go_copies, 1),
     }
-    for name in ORDER:
-        next(streams[name])
+    for names in ORDER:
+        for name in names:
+            next(streams[name])
 
     @pl.when(pipe == 0)
     def _():
         att_cross.wait_send()
 
-    def add_halves(k, carry):
-        rows = rows_of(k * 256, 256)
-        go_ref[rows, :] = (go_own[rows, :] + go_in[rows, :].astype(F32)).astype(BF16)
-        return carry
-
     for one in go_copies:
         one.wait()
-    lax.fori_loop(0, 16, add_halves, 0)
+    keep.wait()
     gv_copy.wait()
     gg_copy.wait()
     gv_ref[...] = (gv_own[...] + gv_in[...].astype(F32)).astype(BF16)
     gg_ref[...] = jnp.sum(gg_own[...] + gg_in[...], axis=0, keepdims=True)
 
 
+def add_halves(own_ref, other_ref, value_ref, gain_ref, go_ref, gv_ref, gg_ref):
+    go_ref[...] = (own_ref[...].astype(F32) + other_ref[...].astype(F32)).astype(BF16)
+
+    @pl.when(pl.program_id(0) == 0)
+    def _():
+        gv_ref[...] = value_ref[...]
+        gg_ref[...] = gain_ref[...]
+
+
 def shards(
     layer_inputs, norm_gain, value_weight, out_weight, scores, head_weight, lengths, returns,
     response_mask,
 ):
-    replica = lax.axis_index("dp")
-    own_lengths = lax.dynamic_index_in_dim(lengths, replica, 0, keepdims=False)
-    attention = attention_weights(scores[0, 0], own_lengths)
-    packed = attention.reshape(2, 2, 2, 4, 32, 32).transpose(0, 3, 4, 2, 1, 5).reshape(2, 128, 128)
-    position = jnp.arange(128, dtype=jnp.int32)
-    block_len = jnp.repeat(own_lengths, 32, total_repeat_length=128)
-    live = ((position % 32 < block_len) & (response_mask == 1)).astype(F32)
-    high = returns.astype(BF16)
-    rest = returns - high.astype(F32)
-    middle = rest.astype(BF16)
-    low = (rest - middle.astype(F32)).astype(BF16)
-    extra = jnp.stack([high, middle, low, live.astype(BF16)])
-    extra = jnp.concatenate([extra, jnp.zeros((12, 128), BF16)], axis=0)
-    packet = jnp.concatenate([packed, jnp.broadcast_to(extra, (2, 16, 128))], axis=1)
-
     vmem = pl.BlockSpec(memory_space=pltpu.VMEM)
     anywhere = pl.BlockSpec(memory_space=pl.ANY)
+    smem = pl.BlockSpec(memory_space=pltpu.SMEM)
 
     def scratch(*shape, dtype=BF16):
         return pltpu.VMEM(shape, dtype)
 
-    grad_out, grad_value, grad_gain = pl.pallas_call(
+    own_out, other_out, grad_value, grad_gain = pl.pallas_call(
         kernel,
         out_shape=(
+            jax.ShapeDtypeStruct((4096, 128), BF16),
             jax.ShapeDtypeStruct((4096, 128), BF16),
             jax.ShapeDtypeStruct((128, 512), BF16),
             jax.ShapeDtypeStruct((1, 128), F32),
         ),
-        in_specs=[vmem, vmem, vmem, anywhere, anywhere, vmem],
-        out_specs=(vmem, vmem, vmem),
+        in_specs=[vmem, smem, vmem, vmem, vmem, vmem, anywhere, anywhere, vmem],
+        out_specs=(anywhere, anywhere, vmem, vmem),
         scratch_shapes=[
+            scratch(2, 144, 128),
             scratch(2, 2, 4, 4, 2, 144, 128),
             scratch(2, 2, 4, 4, 32, 640),
             scratch(2, 1024, 128),
-            scratch(4, 2, 4, 4, 32, 512),
+            scratch(2, 2, 4, 4, 32, 512),
             scratch(4, 4, 32, 512),
             scratch(4, 4, 4, 32, 512),
             scratch(4, 3, 4, 32, 512),
@@ -702,7 +745,6 @@
             scratch(2, 1024, 512),
             scratch(2, 4, 128, 1024),
             scratch(2, 128, 1024),
-            scratch(4096, 128, dtype=F32),
             scratch(4096, 128),
             scratch(4096, 128),
             scratch(128, 512, dtype=F32),
@@ -713,7 +755,7 @@
             scratch(8, 128, dtype=F32),
             pltpu.SemaphoreType.DMA((COPIES,)),
             pltpu.SemaphoreType.DMA((COPIES,)),
-            pltpu.SemaphoreType.DMA((2,)),
+            pltpu.SemaphoreType.DMA((3,)),
         ],
         compiler_params=pltpu.CompilerParams(
             collective_id=0, has_side_effects=True, vmem_limit_bytes=60 * 1024 * 1024
@@ -722,13 +764,30 @@
             flops=8_000_000_000, bytes_accessed=6_000_000, transcendentals=0
         ),
     )(
-        packet,
+        scores[0, 0],
+        lengths.T,
+        returns.reshape(1, 128),
+        response_mask.reshape(1, 128),
         layer_inputs[0],
-        norm_gain[0].reshape(16, 128),
+        norm_gain,
         value_weight[0],
         out_weight[0],
-        head_weight.astype(F32).reshape(16, 128),
+        head_weight.reshape(16, 128),
     )
+    quarter = pl.BlockSpec((1024, 128), lambda k: (k, 0))
+    value_block = pl.BlockSpec((128, 512), lambda k: (0, 0))
+    gain_block = pl.BlockSpec((1, 128), lambda k: (0, 0))
+    grad_out, grad_value, grad_gain = pl.pallas_call(
+        add_halves,
+        out_shape=(
+            jax.ShapeDtypeStruct((4096, 128), BF16),
+            jax.ShapeDtypeStruct((128, 512), BF16),
+            jax.ShapeDtypeStruct((1, 128), F32),
+        ),
+        grid=(4,),
+        in_specs=[quarter, quarter, value_block, gain_block],
+        out_specs=(quarter, value_block, gain_block),
+    )(own_out, other_out, grad_value, grad_gain)
     return grad_out[None], grad_value[None], grad_gain
 
 

time: 181 us -> 170 us (0.939)
  other arithmetic: 9.16 us -> 0 us
  local copies, waits for them, and re-layouts: 5.73 us -> 0 us
  Pallas kernels: 165 us -> 169 us
    another operation x2 -> x0, other arithmetic: 3.97 us -> none  [shards(): extra = jnp.stack([high, middle, low, live.astype(BF16)])]
    pallas_call x0 -> x1, Pallas kernels: none -> 3.73 us  [shards(): pl.pallas_call(add_halves, out_shape=(jax.ShapeDtypeStruct((4096, 128), B...]
    unnamed x15 -> x0, local copies, waits for them, and re-layouts: 3.5 us -> none
where the time goes in v3:
time: 170 us
  Pallas kernels  169 us (99%)
    pallas_call x1, Pallas kernels, shards(): pl.pallas_call(kernel, out_shape=(jax.ShapeDtypeStruct((4096, 128), BF16)...  165 us
    pallas_call x1, Pallas kernels, shards(): pl.pallas_call(add_halves, out_shape=(jax.ShapeDtypeStruct((4096, 128), B...  3.73 us

profile of v3, /device:TPU:0, one launch (start us, length us, event | category | flops | bytes accessed | tf_op | source)
XLA Modules:
  0.0 169.8 jit_solution(15516923655645451548)
XLA Ops:
  0.6 165.4 %shard_map.112 = (bf16[4096,128]{1,0:T(8,128)(2,1)}, bf16[4096,128]{1,0:T(8,128)(2,1)}, bf16[128,512]{1,0:T(8,128)(2,1)}, f32[1,128]{1,0:T(1,128)}) custom-call(bf16[4,8,32,32]{3,2,1,0:T(8,128)(2,1)} %bitcast.13, s32[4,16]{1,0:T(4,128)} %bitcast.17, f32[1,128]{1,0:T(1,128)} %bitcast.18, s32[1,128]{1,0:T(1,128)} %bitcast.19, bf16[128,2048]{1,0:T(8,128)(2,1)} %bitcast.12, ...), custom_call_target="tpu_custom_call" | custom-call | flops 8000000000 | bytes 6000000 | tf_op jit(solution)/shard_map/pallas_call | solution.py:702
  166.0 3.7 %shard_map.113 = (bf16[4096,128]{1,0:T(8,128)(2,1)}, bf16[128,512]{1,0:T(8,128)(2,1)}, f32[1,128]{1,0:T(1,128)}) custom-call(bf16[4096,128]{1,0:T(8,128)(2,1)} %get-tuple-element.10.own_ref, bf16[4096,128]{1,0:T(8,128)(2,1)} %get-tuple-element.11.other_ref, bf16[128,512]{1,0:T(8,128)(2,1)} %get-tuple-element.12.value_ref, f32[1,128]{1,0:T(1,128)} %get-tuple-element.13.gain_ref), custom_call_target="tpu_custom_call" | custom-call | tf_op jit(solution)/shard_map/pallas_call | solution.py:780

commit v4 on v3

--- a/solution.py
+++ b/solution.py
@@ -18,24 +18,24 @@
     "maww",
     "m",
     "maw",
-    "mww",
+    "mwws",
     "maws",
-    "mww",
+    "mwws",
     "mw",
     "mbuu",
-    "muug",
+    "muu",
     "muubug",
     "mug",
     "mbg",
     "mubg",
     "moog",
-    "mboug",
+    "mbougg",
     "mgoo",
-    "mooqqq",
+    "mooq",
     "m",
     "moq",
-    "mqq",
-    "mqq",
+    "mqqq",
+    "mqqq",
     "m",
 )
 
@@ -52,8 +52,8 @@
 def kernel(
     score_ref, length_ref, return_ref, mask_ref, x_ref, gain_ref, wv_ref, w_ref, head_ref,
     go_own, go_in, gv_ref, gg_ref,
-    att_own, att_all, v_all, xf, part, sum1, r0, r1, r2, r2x, gr_all,
-    sq, sq_in, bm, att_t, v_bd, up_bd, wb, wq, wvb, wvt, gains, rms_own, rms_all, hid, st, st_in,
+    att_own, att_all, v_all, x_other, xf, part, sum1, r0, r1, r2, r2x, gr_all,
+    sq, sq_in, bm, att_t, v_bd, up_bd, wb, wq, wvb, wvt, gains, rms_all, hid, st, st_in,
     coef, ret, err_at, up, ng, vg, v_t, nrm_t, go_keep, go_send, gv_own, gv_send, gv_in,
     gg_own, gg_send, gg_in,
     send_sems, recv_sems, local_sems,
@@ -111,40 +111,57 @@
     ]
     start(loads)
     barrier = pltpu.get_barrier_semaphore()
-    partners = [{"dp": to} for to in dp_next[1:]] + t_peers + ax_peers[1:]
-    partners += [{"dp": to, "pipe": other} for to in dp_next]
-    partners += [{"tensor": one["tensor"], "pipe": other} for one in t_peers]
+    partners = [{"dp": to} for to in dp_next[1:]] + t_peers + ax_peers[1:] + [pipe_peer]
     for peer in partners:
         pl.semaphore_signal(barrier, inc=1, device_id=peer, device_id_type=MESH)
     pl.semaphore_wait(barrier, len(partners))
 
-    def x_copy(to, device, half):
-        return remote(
-            x_ref.at[rows_of(half * 64, 64), rows_of(to * 128, 128)],
-            xf.at[pipe, rows_of(dp * 64, 64)], device,
-        )
-
-    x_same = [x_copy(to, {"dp": to}, pipe) for to in dp_next[1:]]
-    x_cross = [x_copy(to, {"dp": to, "pipe": other}, other) for to in dp_next]
-
-    def send_x(layer):
+    def x_copies(rows, layer):
+        return [
+            remote(rows.at[:, rows_of(to * 128, 128)], xf.at[layer, rows_of(dp * 64, 64)], {"dp": to})
+            for to in dp_next[1:]
+        ]
+
+    x_half = x_ref.at[rows_of(pipe * 64, 64)]
+    x_cross = remote(x_ref.at[rows_of(other * 64, 64)], x_other, pipe_peer)
+    x_own = x_copies(x_half, pipe)
+    x_more = x_copies(x_other, other)
+    square_copies = [
+        [
+            remote(sq.at[layer, lax.rem(peer["tensor"], 2)], sq_in.at[layer, tensor], peer)
+            for peer in t_peers
+        ]
+        for layer in range(2)
+    ]
+
+    def send_x(layer, rows, copies):
+        start(copies)
+        xf[layer, rows_of(dp * 64, 64), :] = rows[:, rows_of(dp * 128, 128)]
+        for m in range(2):
+            block = rows[m * 32:(m + 1) * 32, :].astype(F32)
+            sq[layer, m] = jnp.broadcast_to(jnp.sum(block * block, axis=1, keepdims=True), (32, 128))
+        sq_in[layer, tensor] = sq[layer, c]
+        start(square_copies[layer])
+
+    def send_own_x(layer):
         @pl.when(pipe == layer)
         def _():
-            start(x_cross)
-            start(x_same)
-            xf[layer, rows_of(dp * 64, 64), :] = x_ref[rows_of(layer * 64, 64), rows_of(dp * 128, 128)]
+            send_x(layer, x_half, x_own)
+
+    def send_other_x(layer):
+        @pl.when(pipe != layer)
+        def _():
+            x_cross.wait_recv()
+            send_x(layer, x_other, x_more)
 
     def wait_x(layer):
         @pl.when(pipe == layer)
         def _():
-            finish(x_same)
-            for one in x_cross:
-                one.wait_send()
+            finish(x_own)
 
         @pl.when(pipe != layer)
         def _():
-            for one in x_cross:
-                one.wait_recv()
+            finish(x_more)
 
     att_cross = remote(att_own.at[other], att_all.at[pipe, c, a, b, xh], pipe_peer)
 
@@ -278,7 +295,9 @@
         wait_x(layer)
         project(layer)
         yield from scatter(layer, layer)
-        rms = rms_own[layer, :, 0:1]
+        finish(square_copies[layer])
+        squared = sq_in[layer, 0] + sq_in[layer, 1] + sq_in[layer, 2] + sq_in[layer, 3]
+        rms = lax.rsqrt(squared / D + EPS)[:, 0:1]
         total = scattered(layer) * rms
         high, low = split_pair(rms)
         place = lax.broadcasted_iota(jnp.int32, (32, 128), 1)
@@ -574,30 +593,21 @@
         prepare(0)
         yield
 
+    @pl.when(pipe == 1)
+    def _():
+        x_cross.start()
+
     gains[pipe, 0:8, :] = jnp.broadcast_to(gain_ref[:, rows_of(dp * 128, 128)], (8, 128))
     loads[0].wait()
-    cross = [
+    cross = start([
         remote(gains.at[pipe], gains.at[pipe], pipe_peer),
         remote(wvb.at[pipe], wvb.at[pipe], pipe_peer),
-    ]
-    send_x(1)
-    start(cross)
+    ])
+    send_own_x(1)
     attend()
     att_cross.start()
     att_all[pipe, c, a, b, xh] = att_own[pipe]
-    for m in range(4):
-        rows = x_ref[m * 32:(m + 1) * 32, :].astype(F32)
-        sq[m] = jnp.broadcast_to(jnp.sum(rows * rows, axis=1, keepdims=True), (32, 128))
-    sq_in[pipe, tensor] = sq[pipe * 2 + c]
-    squares = []
-    for peer in t_peers:
-        own = lax.rem(peer["tensor"], 2)
-        squares.append(remote(sq.at[pipe * 2 + own], sq_in.at[pipe, tensor], peer))
-        squares.append(remote(
-            sq.at[other * 2 + own], sq_in.at[pipe, tensor], {"tensor": peer["tensor"], "pipe": other}
-        ))
-    squares.append(remote(sq.at[other * 2 + c], sq_in.at[pipe, tensor], pipe_peer))
-    start(squares)
+    send_other_x(1)
     attention1 = gather_attention(1)
     next(attention1)
     loads[1].wait()
@@ -613,10 +623,6 @@
 
     v_bd[...] = jnp.zeros_like(v_bd)
     up_bd[...] = jnp.zeros_like(up_bd)
-    finish(squares)
-    for layer in range(2):
-        squared = sq_in[layer, 0] + sq_in[layer, 1] + sq_in[layer, 2] + sq_in[layer, 3]
-        rms_own[layer] = lax.rsqrt(squared / D + EPS)
     finish(cross)
     next(attention1)
 
@@ -653,13 +659,20 @@
         turn_w(layer)
         yield
 
-    def send_other_x():
-        send_x(0)
+    def other_x():
+        @pl.when(pipe == 0)
+        def _():
+            x_cross.start()
+
+        yield
+        send_own_x(0)
+        yield
+        send_other_x(0)
         yield
 
     streams = {
         "m": main(), "g": background(), "a": attention1, "b": gather_attention(0),
-        "w": weights(1), "u": weights(0), "s": send_other_x(),
+        "w": weights(1), "u": weights(0), "s": other_x(),
         "o": pieces(go_copies, 0), "q": pieces(go_copies, 1),
     }
     for names in ORDER:
@@ -669,6 +682,8 @@
     @pl.when(pipe == 0)
     def _():
         att_cross.wait_send()
+
+    x_cross.wait_send()
 
     for one in go_copies:
         one.wait()
@@ -713,6 +728,7 @@
             scratch(2, 144, 128),
             scratch(2, 2, 4, 4, 2, 144, 128),
             scratch(2, 2, 4, 4, 32, 640),
+            scratch(64, 2048),
             scratch(2, 1024, 128),
             scratch(2, 2, 4, 4, 32, 512),
             scratch(4, 4, 32, 512),
@@ -721,7 +737,7 @@
             scratch(4, 3, 32, 512),
             scratch(4, 4, 32, 512),
             scratch(2, 2, 4, 4, 32, 512),
-            scratch(4, 32, 128, dtype=F32),
+            scratch(2, 2, 32, 128, dtype=F32),
             scratch(2, 4, 32, 128, dtype=F32),
             scratch(2, 1024, 4096),
             scratch(2, 16, 2, 256, 128),
@@ -732,7 +748,6 @@
             scratch(2, 128, 512),
             scratch(2, 512, 128),
             scratch(2, 8, 128, dtype=F32),
-            scratch(2, 32, 128, dtype=F32),
             scratch(2, 1024, 128, dtype=F32),
             scratch(1024, 128, dtype=F32),
             scratch(4, 16, 128, dtype=F32),

time: 170 us -> 170 us (level)
  no operation moved by 1% of the time
where the time goes in v4:
time: 170 us
  Pallas kernels  169 us (99%)
    pallas_call x1, Pallas kernels, shards(): pl.pallas_call(kernel, out_shape=(jax.ShapeDtypeStruct((4096, 128), BF16)...  165 us
    pallas_call x1, Pallas kernels, shards(): pl.pallas_call(add_halves, out_shape=(jax.ShapeDtypeStruct((4096, 128), B...  3.73 us

profile of v4, /device:TPU:0, one launch (start us, length us, event | category | flops | bytes accessed | tf_op | source)
XLA Modules:
  0.0 169.8 jit_solution(5214643068227594042)
XLA Ops:
  0.6 165.4 %shard_map.112 = (bf16[4096,128]{1,0:T(8,128)(2,1)}, bf16[4096,128]{1,0:T(8,128)(2,1)}, bf16[128,512]{1,0:T(8,128)(2,1)}, f32[1,128]{1,0:T(1,128)}) custom-call(bf16[4,8,32,32]{3,2,1,0:T(8,128)(2,1)} %bitcast.13, s32[4,16]{1,0:T(4,128)} %bitcast.17, f32[1,128]{1,0:T(1,128)} %bitcast.18, s32[1,128]{1,0:T(1,128)} %bitcast.19, bf16[128,2048]{1,0:T(8,128)(2,1)} %bitcast.12, ...), custom_call_target="tpu_custom_call" | custom-call | flops 8000000000 | bytes 6000000 | tf_op jit(solution)/shard_map/pallas_call | solution.py:717
  166.0 3.7 %shard_map.113 = (bf16[4096,128]{1,0:T(8,128)(2,1)}, bf16[128,512]{1,0:T(8,128)(2,1)}, f32[1,128]{1,0:T(1,128)}) custom-call(bf16[4096,128]{1,0:T(8,128)(2,1)} %get-tuple-element.10.own_ref, bf16[4096,128]{1,0:T(8,128)(2,1)} %get-tuple-element.11.other_ref, bf16[128,512]{1,0:T(8,128)(2,1)} %get-tuple-element.12.value_ref, f32[1,128]{1,0:T(1,128)} %get-tuple-element.13.gain_ref), custom_call_target="tpu_custom_call" | custom-call | tf_op jit(solution)/shard_map/pallas_call | solution.py:795

commit v5 on v3

--- a/solution.py
+++ b/solution.py
@@ -31,11 +31,11 @@
     "moog",
     "mboug",
     "mgoo",
-    "mooqqq",
+    "mooq",
     "m",
     "moq",
-    "mqq",
-    "mqq",
+    "mqqq",
+    "mqqq",
     "m",
 )
 
@@ -774,7 +774,7 @@
         out_weight[0],
         head_weight.reshape(16, 128),
     )
-    quarter = pl.BlockSpec((1024, 128), lambda k: (k, 0))
+    piece = pl.BlockSpec((2048, 128), lambda k: (k, 0))
     value_block = pl.BlockSpec((128, 512), lambda k: (0, 0))
     gain_block = pl.BlockSpec((1, 128), lambda k: (0, 0))
     grad_out, grad_value, grad_gain = pl.pallas_call(
@@ -784,9 +784,9 @@
             jax.ShapeDtypeStruct((128, 512), BF16),
             jax.ShapeDtypeStruct((1, 128), F32),
         ),
-        grid=(4,),
-        in_specs=[quarter, quarter, value_block, gain_block],
-        out_specs=(quarter, value_block, gain_block),
+        grid=(2,),
+        in_specs=[piece, piece, value_block, gain_block],
+        out_specs=(piece, value_block, gain_block),
     )(own_out, other_out, grad_value, grad_gain)
     return grad_out[None], grad_value[None], grad_gain
 

time: 170 us -> 168 us (0.988)
  Pallas kernels: 169 us -> 167 us
where the time goes in v5:
time: 168 us
  Pallas kernels  167 us (99%)
    pallas_call x1, Pallas kernels, shards(): pl.pallas_call(kernel, out_shape=(jax.ShapeDtypeStruct((4096, 128), BF16)...  165 us

profile of v5, /device:TPU:0, one launch (start us, length us, event | category | flops | bytes accessed | tf_op | source)
XLA Modules:
  0.0 168.1 jit_solution(3211077132990100660)
XLA Ops:
  0.6 164.9 %shard_map.112 = (bf16[4096,128]{1,0:T(8,128)(2,1)}, bf16[4096,128]{1,0:T(8,128)(2,1)}, bf16[128,512]{1,0:T(8,128)(2,1)}, f32[1,128]{1,0:T(1,128)}) custom-call(bf16[4,8,32,32]{3,2,1,0:T(8,128)(2,1)} %bitcast.13, s32[4,16]{1,0:T(4,128)} %bitcast.17, f32[1,128]{1,0:T(1,128)} %bitcast.18, s32[1,128]{1,0:T(1,128)} %bitcast.19, bf16[128,2048]{1,0:T(8,128)(2,1)} %bitcast.12, ...), custom_call_target="tpu_custom_call" | custom-call | flops 8000000000 | bytes 6000000 | tf_op jit(solution)/shard_map/pallas_call | solution.py:702
  165.5 2.5 %shard_map.113 = (bf16[4096,128]{1,0:T(8,128)(2,1)}, bf16[128,512]{1,0:T(8,128)(2,1)}, f32[1,128]{1,0:T(1,128)}) custom-call(bf16[4096,128]{1,0:T(8,128)(2,1)} %get-tuple-element.10.own_ref, bf16[4096,128]{1,0:T(8,128)(2,1)} %get-tuple-element.11.other_ref, bf16[128,512]{1,0:T(8,128)(2,1)} %get-tuple-element.12.value_ref, f32[1,128]{1,0:T(1,128)} %get-tuple-element.13.gain_ref), custom_call_target="tpu_custom_call" | custom-call | tf_op jit(solution)/shard_map/pallas_call | solution.py:780
